TPU v7x, 32 devices: a whole 2x2x4 slice. The times are simulated.
32 devices in a mesh: layers: 2 (over y), row: 4 (over x, core), col: 4 (over z).
Axes of the slice: x: 2, y: 2, z: 4, core: 2. Of those that a mesh axis runs over, the one named last changes fastest.
Arguments:
- factor: bfloat16 [28672, 14336], P(('layers', 'col'), 'row'), parts along dimension 0, may hold values from -1 to 6
- basis_rows: float32 [2048, 14336], P(('layers', 'col'), 'row'), parts along dimension 0, may hold values from -1 to 1
Outputs:
- new_basis: float32 [28672, 1024], P(('layers', 'col'), 'row'), parts along dimension 0
- scales: float32 [2048], P('layers'), parts along dimension 0
There are 2 independent parts, one for each index of `layers`. A program takes and returns all parts, laid end to end along the dimension named above; each array names one. Nothing has to cross between parts.
All inputs are finite; a program needn't handle non-finite values.
Results may differ from a plain program's by a relative error of at most 0.0035.
Values may be sent and summed in bfloat16 or wider, within the bound.
No kernel may reach another device: no remote copies, remote signals or barrier semaphores. Data moves between devices by JAX's collectives and lax.ppermute only.
A program may use at most 256 MiB of HBM per device.

v0:
```python
import math

import jax
import jax.numpy as jnp
from jax import lax
from jax.sharding import PartitionSpec as P

ORDER = 14336
BASIS = 1024


def local(factor, basis_rows):
    rounded = basis_rows.astype(jnp.bfloat16)
    products = lax.dot_general(
        factor,
        lax.all_gather(rounded, "col", axis=0, tiled=True),
        (((1,), (1,)), ((), ())),
        preferred_element_type=jnp.float32,
    )
    portion = BASIS // lax.axis_size("row")
    own_block = lax.psum_scatter(products, "row", scatter_dimension=1, tiled=True)
    rows_full = lax.all_gather(own_block, "row", axis=1, tiled=True)
    partial_value = lax.dot_general(
        own_block,
        rows_full,
        (((0,), (0,)), ((), ())),
        precision=lax.Precision.HIGHEST,
        preferred_element_type=jnp.float32,
    )
    summed = lax.psum(partial_value, "col")
    gram = lax.all_gather(summed, "row", axis=0, tiled=True)
    lower_factor = jnp.linalg.cholesky(gram)
    solved = jax.scipy.linalg.solve_triangular(lower_factor, rows_full.T, lower=True)
    own_columns = lax.dynamic_slice_in_dim(solved, lax.axis_index("row") * portion, portion, 0)
    return (math.sqrt(ORDER) * own_columns.T, jnp.diagonal(lower_factor))


def solution(mesh):
    return jax.shard_map(
        local,
        mesh=mesh,
        in_specs=(P(("layers", "col"), "row"), P(("layers", "col"), "row")),
        out_specs=(P(("layers", "col"), "row"), P("layers")),
        check_vma=False,
    )
```

profile of v0, /device:TPU:0, one launch (start us, length us, event | category | flops | bytes accessed | tf_op | source)
XLA Modules:
  0.0 1000.4 jit_solution(3472911421368681219)
XLA Ops:
  10.7 135.3 %all-gather.4.cloned.1.call-done = bf16[1024,3584]{1,0:T(8,128)(2,1)} async-done(((bf16[256,3584]{1,0:T(8,128)(2,1)}), bf16[1024,3584]{1,0:T(8,128)(2,1)}) %all-gather.4.cloned.1.call-update) | async-done | bytes 7340048 | tf_op jit(solution)/shard_map/all_gather | solution.py:16
  146.0 34.1 %fusion.71 = f32[3584,1024]{1,0:T(8,128)} fusion(bf16[3584,3584]{1,0:T(8,128)(2,1)} %param.2, bf16[1024,3584]{1,0:T(8,128)(2,1)} %all-gather.4.cloned.1.call-done), kind=kOutput, calls=%fused_computation.161 | convolution fusion | flops 26306674688 | bytes 47710208 | tf_op jit(solution)/shard_map/dot_general | solution.py:14
  180.2 111.3 %reduce-scatter.2.cloned.1.call-done = f32[3584,256]{1,0:T(8,128)} async-done(((f32[3584,1024]{1,0:T(8,128)}), f32[3584,256]{1,0:T(8,128)}) %reduce-scatter.2.cloned.1.call-update) | async-done | bytes 3670032 | tf_op jit(solution)/shard_map/reduce_scatter | solution.py:21
  291.8 95.4 %all-gather.6.cloned.1.call-done = f32[3584,1024]{1,0:T(8,128)} async-done(((f32[3584,256]{1,0:T(8,128)}), f32[3584,1024]{1,0:T(8,128)}) %all-gather.6.cloned.1.call-update) | async-done | bytes 14680080 | tf_op jit(solution)/shard_map/all_gather | solution.py:22
  387.1 27.7 %fusion.72 = f32[256,1024]{0,1:T(8,128)} fusion(f32[3584,256]{1,0:T(8,128)} %reduce-scatter.2.cloned.1.call-done, f32[3584,1024]{1,0:T(8,128)} %all-gather.6.cloned.1.call-done), kind=kOutput, calls=%fused_computation.162 | convolution fusion | flops 11274289152 | bytes 19398656 | tf_op jit(solution)/shard_map/dot_general | solution.py:23
  415.0 51.9 %all-reduce.3.cloned.1.call-done = f32[256,1024]{0,1:T(8,128)} async-done(((f32[256,1024]{0,1:T(8,128)}), f32[256,1024]{0,1:T(8,128)}) %all-reduce.3.cloned.1.call-update) | async-done | bytes 1048592 | tf_op jit(solution)/shard_map/psum | solution.py:30
  467.0 35.3 %all-gather.8.cloned.1.call-done = f32[1024,1024]{0,1:T(8,128)} async-done(((f32[256,1024]{0,1:T(8,128)}), f32[1024,1024]{0,1:T(8,128)}) %all-gather.8.cloned.1.call-update) | async-done | bytes 4194320 | tf_op jit(solution)/shard_map/all_gather | solution.py:31
  514.3 11.7 %cholesky.223 = f32[128,128]{1,0:T(8,128)S(1)} custom-call(f32[128,128]{1,0:T(8,128)S(1)} %cholesky.580), custom_call_target="Cholesky" | custom-call | tf_op jit(solution)/shard_map/jit(cholesky)/cholesky | solution.py:32
  526.0 9.8 custom-call.63
  542.3 12.1 %cholesky.244 = f32[128,128]{1,0:T(8,128)S(1)} custom-call(f32[128,128]{1,0:T(8,128)S(1)} %cholesky.584), custom_call_target="Cholesky" | custom-call | tf_op jit(solution)/shard_map/jit(cholesky)/cholesky | solution.py:32
  555.0 9.8 custom-call.64
  568.2 11.7 %cholesky.468 = f32[128,128]{1,0:T(8,128)S(1)} custom-call(f32[128,128]{1,0:T(8,128)S(1)} %cholesky.589), custom_call_target="Cholesky" | custom-call | tf_op jit(solution)/shard_map/jit(cholesky)/cholesky | solution.py:32
  581.3 9.8 custom-call.65
  594.7 11.8 %cholesky.487 = f32[128,128]{1,0:T(8,128)S(1)} custom-call(f32[128,128]{1,0:T(8,128)S(1)} %cholesky.594), custom_call_target="Cholesky" | custom-call | tf_op jit(solution)/shard_map/jit(cholesky)/cholesky | solution.py:32
  607.8 9.8 custom-call.66
  621.1 11.7 %cholesky.506 = f32[128,128]{1,0:T(8,128)S(1)} custom-call(f32[128,128]{1,0:T(8,128)S(1)} %cholesky.599), custom_call_target="Cholesky" | custom-call | tf_op jit(solution)/shard_map/jit(cholesky)/cholesky | solution.py:32
  634.1 10.0 custom-call.67
  647.4 11.7 %cholesky.526 = f32[128,128]{1,0:T(8,128)S(1)} custom-call(f32[128,128]{1,0:T(8,128)S(1)} %cholesky.604), custom_call_target="Cholesky" | custom-call | tf_op jit(solution)/shard_map/jit(cholesky)/cholesky | solution.py:32
  660.4 9.8 custom-call.68
  673.2 12.1 %cholesky.546 = f32[128,128]{1,0:T(8,128)S(1)} custom-call(f32[128,128]{1,0:T(8,128)S(1)} %cholesky.609), custom_call_target="Cholesky" | custom-call | tf_op jit(solution)/shard_map/jit(cholesky)/cholesky | solution.py:32
  686.7 9.8 custom-call.69
  699.2 11.7 %cholesky.564 = f32[128,128]{1,0:T(8,128)S(1)} custom-call(f32[128,128]{1,0:T(8,128)S(1)} %convolution_subtract_fusion.11), custom_call_target="Cholesky" | custom-call | tf_op jit(solution)/shard_map/jit(cholesky)/cholesky | solution.py:32
  724.7 23.5 %while.1 = (s32[]{:T(128)}, f32[1024,1024]{1,0:T(8,128)}, s32[8,2]{0,1:T(2,128)S(1)}, f32[8,128,128]{2,1,0:T(8,128)S(1)}, s32[]{:T(128)}) while((s32[]{:T(128)}, f32[1024,1024]{1,0:T(8,128)}, s32[8,2]{0,1:T(2,128)S(1)}, f32[8,128,128]{2,1,0:T(8,128)S(1)}, s32[]{:T(128)}) %tuple.64), condition=%wide.while_cond, body=%wide.while_body.sunk | while | flops 2 | bytes 131189 | solution.py:33
  748.3 78.8 %custom-call.70 = f32[8,128,128]{1,2,0:T(8,128)S(1)} custom-call(f32[8,128,128]{2,1,0:T(8,128)S(1)} %get-tuple-element.9), custom_call_target="InvertDiagBlocksLowerTriangular" | custom-call | tf_op jit(solution)/shard_map/jit(_solve_triangular)/triangular_solve | solution.py:33
  827.1 6.7 constant_dynamic-update-slice_fusion.17
  843.6 7.3 convolution_subtract_fusion.3
  856.0 10.6 %fusion.14 = f32[128,3584]{0,1:T(8,128)S(1)} fusion(f32[128,3584]{1,0:T(8,128)S(1)} %get-tuple-element.77, f32[128,3584]{1,0:T(8,128)S(1)} %get-tuple-element.76, f32[128,3584]{1,0:T(8,128)S(1)} %get-tuple-element.75, f32[1024,3584]{0,1:T(8,128)S(1)} %bitcast.115, f32[1024,1024]{1,0:T(8,128)} %get-tuple-element.137), kind=kOutput, calls=%fused_computation.23 | convolution fusion | flops 2117140480 | bytes 9371648 | tf_op jit(solution)/shard_map/jit(_solve_triangular)/triangular_solve | solution.py:33
  871.7 13.3 %fusion.17 = f32[128,3584]{0,1:T(8,128)S(1)} fusion(f32[128,3584]{1,0:T(8,128)S(1)} %get-tuple-element.78, f32[128,3584]{1,0:T(8,128)S(1)} %get-tuple-element.77, f32[128,3584]{1,0:T(8,128)S(1)} %get-tuple-element.76, f32[128,3584]{1,0:T(8,128)S(1)} %get-tuple-element.75, f32[1024,3584]{0,1:T(8,128)S(1)} %bitcast.116, f32[1024,1024]{1,0:T(8,128)} %get-tuple-element.137), kind=kOutput, calls=%fused_computation.24 | convolution fusion | flops 2824536064 | bytes 11272192 | tf_op jit(solution)/shard_map/jit(_solve_triangular)/triangular_solve | solution.py:33
  889.9 17.4 %convolution_subtract_fusion.2 = f32[128,3584]{0,1:T(8,128)S(1)} fusion(f32[640,3584]{1,0:T(8,128)} %get-tuple-element.34, f32[1024,3584]{0,1:T(8,128)S(1)} %bitcast.117, f32[1024,1024]{1,0:T(8,128)} %get-tuple-element.137), kind=kOutput, calls=%fused_computation.20 | convolution fusion | flops 3523674112 | bytes 13172736 | tf_op jit(solution)/shard_map/jit(_solve_triangular)/triangular_solve | solution.py:33
  911.6 20.9 %convolution_subtract_fusion.1 = f32[128,3584]{0,1:T(8,128)S(1)} fusion(f32[768,3584]{1,0:T(8,128)} %get-tuple-element.30, f32[1024,3584]{0,1:T(8,128)S(1)} %bitcast.118, f32[1024,1024]{1,0:T(8,128)} %get-tuple-element.137), kind=kOutput, calls=%fused_computation.19 | convolution fusion | flops 4228317184 | bytes 15073280 | tf_op jit(solution)/shard_map/jit(_solve_triangular)/triangular_solve | solution.py:33
  936.1 24.1 %convolution_subtract_fusion = f32[128,3584]{0,1:T(8,128)S(1)} fusion(f32[896,3584]{1,0:T(8,128)} %get-tuple-element.26, f32[1024,3584]{0,1:T(8,128)S(1)} %bitcast.119, f32[1024,1024]{1,0:T(8,128)} %get-tuple-element.137), kind=kOutput, calls=%fused_computation.18 | convolution fusion | flops 4932960256 | bytes 16973824 | tf_op jit(solution)/shard_map/jit(_solve_triangular)/triangular_solve | solution.py:33
  972.4 21.3 %gather_fusion = f32[1024]{0:T(1024)} fusion(f32[1024,1024]{1,0:T(8,128)} %get-tuple-element.23, s32[1024]{0:T(1024)S(1)} %bitcast.109), kind=kCustom, calls=%fused_computation | custom fusion | bytes 16384 | tf_op jit(solution)/shard_map/jit(diagonal)/cond/branch_0_fun/gather | solution.py:35
  (100 shorter events, 126.0 us)
Async XLA Ops:
  7.2 138.9 %all-gather.4.cloned.1.call-start = ((), (), s32[]{:S(2)}) async-start(), calls=%async_computation.1 | async-start | bytes 9175040 | tf_op jit(solution)/shard_map/all_gather | solution.py:16
  10.7 280.8 %reduce-scatter.2.cloned.1.call-start = ((), (), s32[]{:S(2)}) async-start(), calls=%async_computation.2 | async-start | bytes 18350080 | tf_op jit(solution)/shard_map/reduce_scatter | solution.py:21
  180.2 207.0 %all-gather.6.cloned.1.call-start = ((), (), s32[]{:S(2)}) async-start(), calls=%async_computation.3 | async-start | bytes 18350080 | tf_op jit(solution)/shard_map/all_gather | solution.py:22
  291.5 175.4 %all-reduce.3.cloned.1.call-start = ((), (), s32[]{:S(2)}) async-start(), calls=%async_computation.4 | async-start | bytes 2097152 | tf_op jit(solution)/shard_map/psum | solution.py:30
  414.9 87.4 %all-gather.8.cloned.1.call-start = ((), (), s32[]{:S(2)}) async-start(), calls=%async_computation.5 | async-start | bytes 5242880 | tf_op jit(solution)/shard_map/all_gather | solution.py:31
  512.3 2.0 copy-start
  827.1 16.5 %slice-start = ((s8[14680064]{0:T(1024)(128)(4,1)}), s8[4194304]{0:T(1024)(128)(4,1)S(1)}, s32[]{:S(2)}) async-start(s8[14680064]{0:T(1024)(128)(4,1)} %bitcast.112), calls=%async_computation.6 | async-start | bytes 8388608
  827.1 16.5 %slice-start.1 = ((s8[14680064]{0:T(1024)(128)(4,1)}), s8[4194304]{0:T(1024)(128)(4,1)S(1)}, s32[]{:S(2)}) async-start(s8[14680064]{0:T(1024)(128)(4,1)} %bitcast.112), calls=%async_computation.7 | async-start | bytes 8388608
  833.8 9.8 slice-start.2
  838.5 5.0 slice-start.3
Sparse Core Ops, SparseCore 0:
  10.8 135.1 all-gather.3
  180.3 111.1 reduce-scatter.1
  293.1 94.0 all-gather.5
  415.0 51.8 all-reduce.2
  468.4 33.8 all-gather.7
where the time goes:
time: 1010 us; the launch traced here: 1000 us
  waiting for transfers between devices  429 us (42%)
  other arithmetic  270 us (27%)
  matrix products  221 us (22%)
  local copies, waits for them, and re-layouts  60 us (6%)
  between operations  19.4 us (2%)
    another operation x30, other arithmetic, local(): lower_factor = jnp.linalg.cholesky(gram)  173 us
    another operation x15, matrix products, local(): jax.scipy.linalg.solve_triangular(lower_factor, rows_full.T, lower=True)  136 us
    all_gather x1, waiting for transfers between devices, local(): lax.all_gather(rounded, 'col', axis=0, tiled=True)  135 us
    reduce_scatter x1, waiting for transfers between devices, local(): lax.psum_scatter(products, 'row', scatter_dimension=1, tiled=True)  111 us
    all_gather x1, waiting for transfers between devices, local(): rows_full = lax.all_gather(own_block, 'row', axis=1, tiled=True)  95.4 us
    another operation x3, other arithmetic, local(): jax.scipy.linalg.solve_triangular(lower_factor, rows_full.T, lower=True)  85.4 us
    psum x1, waiting for transfers between devices, local(): summed = lax.psum(partial_value, 'col')  51.9 us
    all_gather x1, waiting for transfers between devices, local(): gram = lax.all_gather(summed, 'row', axis=0, tiled=True)  35.3 us
  transfers between devices with their start and end apart: 5, of which 5 were waited for; matrix products, arithmetic and copies ran while one was open for 0% of the time, Pallas kernels for 0%

commit v1 on v0

v1 whole, which is shorter than its diff:
```python
import functools
import math

import jax
import jax.numpy as jnp
from jax import lax
from jax.experimental import pallas as pl
from jax.experimental.pallas import tpu as pltpu
from jax.sharding import PartitionSpec as P

ORDER = 14336
BLOCK = 128
STEP = 8
PANEL = 32
EXACT = lax.Precision.HIGHEST


def dot_rows(x, y):
    return lax.dot_general(x, y, (((0,), (0,)), ((), ())), precision=EXACT, preferred_element_type=jnp.float32)


def dot_plain(x, y):
    return lax.dot_general(x, y, (((1,), (0,)), ((), ())), precision=EXACT, preferred_element_type=jnp.float32)


def factor_block(block):
    pieces = BLOCK // 8
    shape = (8, BLOCK)
    row = lax.broadcasted_iota(jnp.int32, shape, 0)
    column = lax.broadcasted_iota(jnp.int32, shape, 1)
    left = [block[8 * i : 8 * i + 8, :] for i in range(pieces)]
    right = [jnp.where(column == row + 8 * i, 1.0, 0.0).astype(jnp.float32) for i in range(pieces)]
    diagonal = jnp.zeros(shape, jnp.float32)

    def spread(value):
        return jnp.broadcast_to(value, shape)

    for first in range(0, BLOCK, STEP):
        own = first // 8
        end = (first // PANEL + 1) * PANEL // 8
        lanes = [spread(left[own][:, first + s : first + s + 1]) for s in range(STEP)]
        corner = [[spread(lanes[t][s : s + 1, :]) if t >= s else None for t in range(STEP)] for s in range(STEP)]
        rows = [spread(left[own][s : s + 1, :]) for s in range(STEP)]
        sides = [spread(right[own][s : s + 1, :]) for s in range(STEP)]
        columns = [
            {i: spread(left[i][:, first + s : first + s + 1]) for i in range(own + 1, end)} for s in range(STEP)
        ]
        ratio, inverse = {}, []
        for s in range(STEP):
            guess = pl.reciprocal(corner[s][s], approx=True)
            inverse.append(guess * (2.0 - corner[s][s] * guess))
            for t in range(s + 1, STEP):
                ratio[t, s] = corner[s][t] * inverse[s]
                for u in range(t, STEP):
                    corner[t][u] = corner[t][u] - ratio[t, s] * corner[s][u]
        for s in range(STEP):
            for t in range(s + 1, STEP):
                rows[t] = rows[t] - ratio[t, s] * rows[s]
                sides[t] = sides[t] - ratio[t, s] * sides[s]
        if own + 1 < end:
            solved_rows, solved_sides = [None] * STEP, [None] * STEP
            for s in reversed(range(STEP)):
                solved_rows[s] = rows[s] * inverse[s]
                solved_sides[s] = sides[s] * inverse[s]
                for t in range(s + 1, STEP):
                    solved_rows[s] = solved_rows[s] - ratio[t, s] * solved_rows[t]
                    solved_sides[s] = solved_sides[s] - ratio[t, s] * solved_sides[t]
            for i in range(own + 1, end):
                for s in range(STEP):
                    left[i] = left[i] - columns[s][i] * solved_rows[s]
                    right[i] = right[i] - columns[s][i] * solved_sides[s]
        for s in range(STEP):
            root = lax.rsqrt(corner[s][s])
            diagonal = jnp.where(column == first + s, corner[s][s] * root, diagonal)
            left[own] = jnp.where(row == s, rows[s] * root, left[own])
            right[own] = jnp.where(row == s, sides[s] * root, right[own])
        if (first + STEP) % PANEL == 0 and first + STEP < BLOCK:
            start = (first + STEP - PANEL) // 8
            upper = jnp.concatenate(left[start:end], axis=0)
            side = jnp.concatenate(right[start:end], axis=0)
            update = dot_rows(upper, jnp.concatenate([upper, side], axis=1))
            for i in range(end, pieces):
                left[i] = left[i] - update[8 * i : 8 * i + 8, :BLOCK]
                right[i] = right[i] - update[8 * i : 8 * i + 8, BLOCK:]
    return right, diagonal[:1]


def factor_kernel(gram_ref, high_ref, low_ref, scales_ref, work):
    size = gram_ref.shape[0]
    blocks = size // BLOCK
    work[...] = gram_ref[...]
    one = lax.broadcasted_iota(jnp.int32, (BLOCK, BLOCK), 0) == lax.broadcasted_iota(jnp.int32, (BLOCK, BLOCK), 1)

    @pl.loop(0, blocks)
    def _(j):
        own = pl.ds(pl.multiple_of(j * BLOCK, BLOCK), BLOCK)
        pieces, diagonal = factor_block(work[own, own])
        scales_ref[:, own] = diagonal
        work[own, own] = jnp.where(one, 1.0, 0.0).astype(jnp.float32)
        work[own, :] = dot_plain(jnp.concatenate(pieces, axis=0), work[own, :])

        @pl.loop(j + 1, blocks)
        def _(i):
            other = pl.ds(pl.multiple_of(i * BLOCK, BLOCK), BLOCK)
            upper = work[own, other]
            work[other, own] = jnp.zeros((BLOCK, BLOCK), jnp.float32)
            work[other, :] = work[other, :] - dot_rows(upper, work[own, :])

    row = lax.broadcasted_iota(jnp.int32, (size, size), 0)
    column = lax.broadcasted_iota(jnp.int32, (size, size), 1)
    full = jnp.where(column <= row, work[...], 0.0)
    high = full.astype(jnp.bfloat16)
    high_ref[...] = high
    low_ref[...] = (full - high.astype(jnp.float32)).astype(jnp.bfloat16)


def invert_factor(gram):
    size = gram.shape[0]
    vmem = pl.BlockSpec(memory_space=pltpu.VMEM)
    return pl.pallas_call(
        factor_kernel,
        out_shape=[
            jax.ShapeDtypeStruct((size, size), jnp.bfloat16),
            jax.ShapeDtypeStruct((size, size), jnp.bfloat16),
            jax.ShapeDtypeStruct((1, size), jnp.float32),
        ],
        in_specs=[vmem],
        out_specs=[vmem] * 3,
        scratch_shapes=[pltpu.VMEM((size, size), jnp.float32)],
        compiler_params=pltpu.CompilerParams(vmem_limit_bytes=40 * 2**20),
    )(gram)


def local(factor, basis_rows):
    rows, depth = factor.shape
    own_basis = basis_rows.shape[0]
    n_row, n_col = lax.axis_size("row"), lax.axis_size("col")
    basis = own_basis * n_col
    chunks = max(1, min(4, own_basis // 16))
    height = own_basis // chunks
    half = rows // 2
    index = lax.axis_index("row")
    core = index % 2

    def exchange(value, axis, distance):
        size = lax.axis_size(axis)
        return lax.ppermute(value, axis, [(i, i ^ distance) for i in range(size)])

    rounded = basis_rows.astype(jnp.bfloat16)
    parts = []
    for k in range(chunks):
        gathered = lax.all_gather(rounded[k * height : (k + 1) * height], "col", axis=0, tiled=True)
        partial = lax.dot_general(gathered, factor, (((1,), (1,)), ((), ())), preferred_element_type=jnp.float32)
        kept = jnp.where(core == 0, partial[:, :half], partial[:, half:])
        given = jnp.where(core == 0, partial[:, half:], partial[:, :half])
        total = kept + exchange(given, "row", 1)
        distance = 2
        while distance < n_row:
            narrow = total.astype(jnp.bfloat16)
            total = narrow.astype(jnp.float32) + exchange(narrow, "row", distance).astype(jnp.float32)
            distance *= 2
        total = total.astype(jnp.bfloat16)
        other = exchange(total, "row", 1)
        full = jnp.concatenate(
            [jnp.where(core == 0, total, other), jnp.where(core == 0, other, total)], axis=1
        )
        parts.append(full.reshape(n_col, height, rows))
    products = jnp.stack(parts, axis=1).reshape(basis, rows)

    portion = basis // n_row
    own_part = lax.dynamic_slice_in_dim(products, index * portion, portion, 0)
    gram = lax.dot_general(own_part, products, (((1,), (1,)), ((), ())), preferred_element_type=jnp.float32)
    distance = 1
    while distance < n_col:
        gram = gram + exchange(gram, "col", distance)
        distance *= 2
    gram = lax.all_gather(gram, "row", axis=0, tiled=True)
    high, low, scales = invert_factor(gram)
    high = lax.dynamic_slice_in_dim(high, index * portion, portion, 0)
    low = lax.dynamic_slice_in_dim(low, index * portion, portion, 0)
    new_basis = lax.dot_general(
        products, high, (((0,), (1,)), ((), ())), preferred_element_type=jnp.float32
    ) + lax.dot_general(products, low, (((0,), (1,)), ((), ())), preferred_element_type=jnp.float32)
    return (math.sqrt(ORDER) * new_basis, scales[0])


def solution(mesh):
    return jax.shard_map(
        local,
        mesh=mesh,
        in_specs=(P(("layers", "col"), "row"), P(("layers", "col"), "row")),
        out_specs=(P(("layers", "col"), "row"), P("layers")),
        check_vma=False,
    )
```

time: 1010 us -> 478 us (0.47)
  other arithmetic: 270 us -> 28.6 us
  matrix products: 221 us -> 66.8 us
  waiting for transfers between devices: 429 us -> 294 us
  Pallas kernels: 0 us -> 63.1 us
  local copies, waits for them, and re-layouts: 60 us -> 4.27 us
    another operation x33 -> x1, other arithmetic: 258 us -> 0.99 us  [local(): products = jnp.stack(parts, axis=1).reshape(basis, rows)]
    another operation x29 -> x0, matrix products: 159 us -> none  [the longest x15 136 us: local(): jax.scipy.linalg.solve_triangular(lower_factor, rows_full.T, lower=True)]
    ppermute x0 -> x14, waiting for transfers between devices: none -> 143 us  [exchange(): return lax.ppermute(value, axis, [(i, i ^ distance) for i in range(size)])]
    all_gather x3 -> x5, waiting for transfers between devices: 266 us -> 149 us  [the longest x4 115 us: local(): lax.all_gather(rounded[k * height:(k + 1) * height], 'col', axis=0, tiled...]
    reduce_scatter x1 -> x0, waiting for transfers between devices: 111 us -> none  [local(): lax.psum_scatter(products, 'row', scatter_dimension=1, tiled=True)]
    pallas_call x0 -> x1, Pallas kernels: none -> 63.1 us  [invert_factor(): pl.pallas_call(factor_kernel, out_shape=[jax.ShapeDtypeStruct((size, size...]
    psum x1 -> x0, waiting for transfers between devices: 51.9 us -> none  [local(): summed = lax.psum(partial_value, 'col')]
    another operation x33 -> x0, local copies, waits for them, and re-layouts: 26 us -> none
  transfers between devices with their start and end apart: 5 -> 19, of which waited for: 5 -> 12; matrix products, arithmetic and copies ran while one was open for 0% -> 17% of each run, Pallas kernels for 0% -> 0%
where the time goes in v1:
time: 478 us
  waiting for transfers between devices  294 us (62%)
  matrix products  66.8 us (14%)
  Pallas kernels  63.1 us (13%)
  other arithmetic  28.6 us (6%)
  between operations  14 us (3%)
  starting transfers between devices  6.76 us (1%)
    ppermute x14, waiting for transfers between devices, exchange(): return lax.ppermute(value, axis, [(i, i ^ distance) for i in range(size)])  143 us
    all_gather x4, waiting for transfers between devices, local(): lax.all_gather(rounded[k * height:(k + 1) * height], 'col', axis=0, tiled...  115 us
    pallas_call x1, Pallas kernels, invert_factor(): pl.pallas_call(factor_kernel, out_shape=[jax.ShapeDtypeStruct((size, size...  63.1 us
    dot_general x4, matrix products, local(): lax.dot_general(gathered, factor, (((1,), (1,)), ((), ())), preferred_ele...  55.4 us
    all_gather x1, waiting for transfers between devices, local(): gram = lax.all_gather(gram, 'row', axis=0, tiled=True)  33.7 us
    select_n x4, other arithmetic, local(): given = jnp.where(core == 0, partial[:, half:], partial[:, :half])  14.1 us
  transfers between devices with their start and end apart: 19, of which 12 were waited for; matrix products, arithmetic and copies ran while one was open for 17% of the time, Pallas kernels for 0%

profile of v1, /device:TPU:0, one launch (start us, length us, event | category | flops | bytes accessed | tf_op | source)
XLA Modules:
  0.0 477.8 jit_solution(27377972184307298)
XLA Ops:
  7.2 2.2 convert_element_type.51
  12.8 42.1 %all-gather.6.cloned.1.call-done = bf16[256,3584]{1,0:T(8,128)(2,1)} async-done(((bf16[64,3584]{1,0:T(8,128)(2,1)}), bf16[256,3584]{1,0:T(8,128)(2,1)}) %all-gather.6.cloned.1.call-update) | async-done | bytes 1835024 | tf_op jit(solution)/shard_map/all_gather | solution.py:152
  55.0 13.9 %fusion.10 = f32[256,3584]{1,0:T(8,128)} fusion(bf16[256,3584]{1,0:T(8,128)(2,1)} %all-gather.6.cloned.1.call-done, bf16[3584,3584]{1,0:T(8,128)(2,1)} %param.2), kind=kOutput, calls=%fused_computation.36 | convolution fusion | flops 6576668672 | bytes 31195136 | tf_op jit(solution)/shard_map/dot_general | solution.py:153
  68.9 3.5 slice_select_fusion.3
  72.4 24.5 %all-gather.8.cloned.1.call-done = bf16[256,3584]{1,0:T(8,128)(2,1)} async-done(((bf16[64,3584]{1,0:T(8,128)(2,1)}), bf16[256,3584]{1,0:T(8,128)(2,1)}) %all-gather.8.cloned.1.call-update) | async-done | bytes 1835024 | tf_op jit(solution)/shard_map/all_gather | solution.py:152
  96.8 13.9 %fusion.11 = f32[256,3584]{1,0:T(8,128)} fusion(bf16[256,3584]{1,0:T(8,128)(2,1)} %all-gather.8.cloned.1.call-done, bf16[3584,3584]{1,0:T(8,128)(2,1)} %param.2), kind=kOutput, calls=%fused_computation.37 | convolution fusion | flops 6576668672 | bytes 31195136 | tf_op jit(solution)/shard_map/dot_general | solution.py:153
  110.8 3.5 slice_select_fusion.2
  114.3 24.5 %all-gather.10.cloned.1.call-done = bf16[256,3584]{1,0:T(8,128)(2,1)} async-done(((bf16[64,3584]{1,0:T(8,128)(2,1)}), bf16[256,3584]{1,0:T(8,128)(2,1)}) %all-gather.10.cloned.1.call-update) | async-done | bytes 1835024 | tf_op jit(solution)/shard_map/all_gather | solution.py:152
  138.7 13.9 %fusion.12 = f32[256,3584]{1,0:T(8,128)} fusion(bf16[256,3584]{1,0:T(8,128)(2,1)} %all-gather.10.cloned.1.call-done, bf16[3584,3584]{1,0:T(8,128)(2,1)} %param.2), kind=kOutput, calls=%fused_computation.38 | convolution fusion | flops 6576668672 | bytes 31195136 | tf_op jit(solution)/shard_map/dot_general | solution.py:153
  152.7 3.5 slice_select_fusion.1
  156.2 24.3 %all-gather.12.cloned.1.call-done = bf16[256,3584]{1,0:T(8,128)(2,1)} async-done(((bf16[64,3584]{1,0:T(8,128)(2,1)}), bf16[256,3584]{1,0:T(8,128)(2,1)}) %all-gather.12.cloned.1.call-update) | async-done | bytes 1835024 | tf_op jit(solution)/shard_map/all_gather | solution.py:152
  180.5 13.6 %fusion.13 = f32[256,3584]{1,0:T(8,128)} fusion(bf16[256,3584]{1,0:T(8,128)(2,1)} %all-gather.12.cloned.1.call-done, bf16[3584,3584]{1,0:T(8,128)(2,1)} %param.2), kind=kOutput, calls=%fused_computation.39 | convolution fusion | flops 6576668672 | bytes 31195136 | tf_op jit(solution)/shard_map/dot_general | solution.py:153
  194.0 3.6 slice_select_fusion
  197.6 2.5 add_convert_fusion.7
  200.1 1.5 collective-permute-start.1
  201.6 1.9 add_convert_fusion.5
  204.4 2.0 add_convert_fusion.3
  207.5 1.9 add_convert_fusion.1
  210.5 12.8 %collective-permute-done.1 = bf16[256,1792]{1,0:T(8,128)(2,1)S(1)} collective-permute-done((bf16[256,1792]{1,0:T(8,128)(2,1)S(1)}, bf16[256,1792]{1,0:T(8,128)(2,1)S(1)}, u32[]{:S(2)}, u32[]{:S(2)}) %collective-permute-start.1) | collective-permute-done | bytes 917536 | tf_op jit(solution)/shard_map/ppermute | solution.py:147
  223.6 19.4 %collective-permute-done.4 = bf16[256,1792]{1,0:T(8,128)(2,1)S(1)} collective-permute-done((bf16[256,1792]{1,0:T(8,128)(2,1)S(1)}, bf16[256,1792]{1,0:T(8,128)(2,1)S(1)}, u32[]{:S(2)}, u32[]{:S(2)}) %collective-permute-start.4) | collective-permute-done | bytes 917536 | tf_op jit(solution)/shard_map/ppermute | solution.py:147
  243.3 19.4 %collective-permute-done.7 = bf16[256,1792]{1,0:T(8,128)(2,1)S(1)} collective-permute-done((bf16[256,1792]{1,0:T(8,128)(2,1)S(1)}, bf16[256,1792]{1,0:T(8,128)(2,1)S(1)}, u32[]{:S(2)}, u32[]{:S(2)}) %collective-permute-start.7) | collective-permute-done | bytes 917536 | tf_op jit(solution)/shard_map/ppermute | solution.py:147
  262.9 19.0 %collective-permute-done.10 = bf16[256,1792]{1,0:T(8,128)(2,1)S(1)} collective-permute-done((bf16[256,1792]{1,0:T(8,128)(2,1)S(1)}, bf16[256,1792]{1,0:T(8,128)(2,1)S(1)}, u32[]{:S(2)}, u32[]{:S(2)}) %collective-permute-start.10) | collective-permute-done | bytes 917536 | tf_op jit(solution)/shard_map/ppermute | solution.py:147
  283.0 1.6 collective-permute-done.11
  286.0 2.1 fusion.1
  289.1 24.9 %collective-permute-done.12 = f32[256,1024]{1,0:T(8,128)S(1)} collective-permute-done((f32[256,1024]{1,0:T(8,128)S(1)}, f32[256,1024]{1,0:T(8,128)S(1)}, u32[]{:S(2)}, u32[]{:S(2)}) %collective-permute-start.12) | collective-permute-done | bytes 1048608 | tf_op jit(solution)/shard_map/ppermute | solution.py:147
  314.2 1.4 collective-permute-start.13
  315.6 46.2 %collective-permute-done.13 = f32[256,1024]{1,0:T(8,128)S(1)} collective-permute-done((f32[256,1024]{1,0:T(8,128)S(1)}, f32[256,1024]{1,0:T(8,128)S(1)}, u32[]{:S(2)}, u32[]{:S(2)}) %collective-permute-start.13) | collective-permute-done | bytes 1048608 | tf_op jit(solution)/shard_map/ppermute | solution.py:147
  362.9 33.7 %all-gather.14.cloned.1.call-done.gram_ref = f32[1024,1024]{1,0:T(8,128)} async-done(((f32[256,1024]{1,0:T(8,128)}), f32[1024,1024]{1,0:T(8,128)}) %all-gather.14.cloned.1.call-update) | async-done | bytes 4194320 | tf_op jit(solution)/shard_map/all_gather | solution.py:177
  396.6 2.2 copy-done
  398.8 63.1 %shard_map.41 = (bf16[1024,1024]{1,0:T(8,128)(2,1)S(1)}, bf16[1024,1024]{1,0:T(8,128)(2,1)S(1)}, f32[1,1024]{1,0:T(1,128)}) custom-call(f32[1024,1024]{1,0:T(8,128)S(1)} %copy-done), custom_call_target="tpu_custom_call" | custom-call | tf_op jit(solution)/shard_map/pallas_call | solution.py:120
  461.9 5.4 %fusion.4 = f32[3584,256]{1,0:T(8,128)S(1)} fusion(bf16[1024,3584]{1,0:T(8,128)(2,1)} %bitcast.26, bf16[1024,1024]{1,0:T(8,128)(2,1)S(1)} %get-tuple-element.5, s32[]{:T(128)S(6)} %select_n.100), kind=kOutput, calls=%fused_computation.30 | convolution fusion | flops 1879048192 | bytes 11534340 | tf_op jit(solution)/shard_map/dot_general | solution.py:181
  467.3 4.0 fusion
  (59 shorter events, 12.0 us)
Async XLA Ops:
  7.2 47.8 %all-gather.6.cloned.1.call-start = ((), (), s32[]{:S(2)}) async-start(), calls=%async_computation | async-start | bytes 2293760 | tf_op jit(solution)/shard_map/all_gather | solution.py:152
  10.7 86.1 %all-gather.8.cloned.1.call-start = ((), (), s32[]{:S(2)}) async-start(), calls=%async_computation.1 | async-start | bytes 2293760 | tf_op jit(solution)/shard_map/all_gather | solution.py:152
  11.5 127.3 %all-gather.10.cloned.1.call-start = ((), (), s32[]{:S(2)}) async-start(), calls=%async_computation.2 | async-start | bytes 2293760 | tf_op jit(solution)/shard_map/all_gather | solution.py:152
  12.2 168.3 %all-gather.12.cloned.1.call-start = ((), (), s32[]{:S(2)}) async-start(), calls=%async_computation.3 | async-start | bytes 2293760 | tf_op jit(solution)/shard_map/all_gather | solution.py:152
  12.8 383.8 %all-gather.14.cloned.1.call-start = ((), (), s32[]{:S(2)}) async-start(), calls=%async_computation.4 | async-start | bytes 5242880 | tf_op jit(solution)/shard_map/all_gather | solution.py:177
  72.4 125.3 %collective-permute-start = (f32[256,1792]{1,0:T(8,128)}, f32[256,1792]{1,0:T(8,128)S(1)}, u32[]{:S(2)}, u32[]{:S(2)}) collective-permute-start(f32[256,1792]{1,0:T(8,128)} %slice_select_fusion.3), channel_id=1, source_target_pairs={{0,4},{4,0},{8,12},{12,8},{1,5},{5,1},{9,13},{13,9},{2,6},{6,2},{1... | collective-permute-start | bytes 5505032 | tf_op jit(solution)/shard_map/ppermute | solution.py:147
  114.3 87.3 %collective-permute-start.3 = (f32[256,1792]{1,0:T(8,128)}, f32[256,1792]{1,0:T(8,128)}, u32[]{:S(2)}, u32[]{:S(2)}) collective-permute-start(f32[256,1792]{1,0:T(8,128)} %slice_select_fusion.2), channel_id=1, source_target_pairs={{0,4},{4,0},{8,12},{12,8},{1,5},{5,1},{9,13},{13,9},{2,6},{6,2},{1... | collective-permute-start | bytes 5505032 | tf_op jit(solution)/shard_map/ppermute | solution.py:147
  156.2 48.2 %collective-permute-start.6 = (f32[256,1792]{1,0:T(8,128)}, f32[256,1792]{1,0:T(8,128)}, u32[]{:S(2)}, u32[]{:S(2)}) collective-permute-start(f32[256,1792]{1,0:T(8,128)} %slice_select_fusion.1), channel_id=1, source_target_pairs={{0,4},{4,0},{8,12},{12,8},{1,5},{5,1},{9,13},{13,9},{2,6},{6,2},{1... | collective-permute-start | bytes 5505032 | tf_op jit(solution)/shard_map/ppermute | solution.py:147
  197.6 9.9 %collective-permute-start.9 = (f32[256,1792]{1,0:T(8,128)}, f32[256,1792]{1,0:T(8,128)}, u32[]{:S(2)}, u32[]{:S(2)}) collective-permute-start(f32[256,1792]{1,0:T(8,128)} %slice_select_fusion), channel_id=1, source_target_pairs={{0,4},{4,0},{8,12},{12,8},{1,5},{5,1},{9,13},{13,9},{2,6},{6,2},{1... | collective-permute-start | bytes 5505032 | tf_op jit(solution)/shard_map/ppermute | solution.py:147
  197.6 4.0 copy-start.2
  200.1 4.4 copy-start.3
  200.1 23.2 %collective-permute-start.1 = (bf16[256,1792]{1,0:T(8,128)(2,1)S(1)}, bf16[256,1792]{1,0:T(8,128)(2,1)S(1)}, u32[]{:S(2)}, u32[]{:S(2)}) collective-permute-start(bf16[256,1792]{1,0:T(8,128)(2,1)S(1)} %add_convert_fusion.7), channel_id=1, source_target_pairs={{0,8},{4,12},{8,0},{12,4},{1,9},{5,13},{9,1},{13,5},{2,10},{6,14},... | collective-permute-start | bytes 2752520 | tf_op jit(solution)/shard_map/ppermute | solution.py:147
  203.5 4.0 copy-start.4
  203.5 39.5 %collective-permute-start.4 = (bf16[256,1792]{1,0:T(8,128)(2,1)S(1)}, bf16[256,1792]{1,0:T(8,128)(2,1)S(1)}, u32[]{:S(2)}, u32[]{:S(2)}) collective-permute-start(bf16[256,1792]{1,0:T(8,128)(2,1)S(1)} %add_convert_fusion.5), channel_id=1, source_target_pairs={{0,8},{4,12},{8,0},{12,4},{1,9},{5,13},{9,1},{13,5},{2,10},{6,14},... | collective-permute-start | bytes 2752520 | tf_op jit(solution)/shard_map/ppermute | solution.py:147
  206.4 56.2 %collective-permute-start.7 = (bf16[256,1792]{1,0:T(8,128)(2,1)S(1)}, bf16[256,1792]{1,0:T(8,128)(2,1)S(1)}, u32[]{:S(2)}, u32[]{:S(2)}) collective-permute-start(bf16[256,1792]{1,0:T(8,128)(2,1)S(1)} %add_convert_fusion.3), channel_id=1, source_target_pairs={{0,8},{4,12},{8,0},{12,4},{1,9},{5,13},{9,1},{13,5},{2,10},{6,14},... | collective-permute-start | bytes 2752520 | tf_op jit(solution)/shard_map/ppermute | solution.py:147
  209.4 72.5 %collective-permute-start.10 = (bf16[256,1792]{1,0:T(8,128)(2,1)S(1)}, bf16[256,1792]{1,0:T(8,128)(2,1)S(1)}, u32[]{:S(2)}, u32[]{:S(2)}) collective-permute-start(bf16[256,1792]{1,0:T(8,128)(2,1)S(1)} %add_convert_fusion.1), channel_id=1, source_target_pairs={{0,8},{4,12},{8,0},{12,4},{1,9},{5,13},{9,1},{13,5},{2,10},{6,14},... | collective-permute-start | bytes 2752520 | tf_op jit(solution)/shard_map/ppermute | solution.py:147
  223.5 58.7 %collective-permute-start.2 = (bf16[256,1792]{1,0:T(8,128)(2,1)S(1)}, bf16[256,1792]{1,0:T(8,128)(2,1)S(1)}, u32[]{:S(2)}, u32[]{:S(2)}) collective-permute-start(bf16[256,1792]{1,0:T(8,128)(2,1)S(1)} %add_convert_fusion.6), channel_id=1, source_target_pairs={{0,4},{4,0},{8,12},{12,8},{1,5},{5,1},{9,13},{13,9},{2,6},{6,2},{1... | collective-permute-start | bytes 2752520 | tf_op jit(solution)/shard_map/ppermute | solution.py:147
  243.2 39.3 %collective-permute-start.5 = (bf16[256,1792]{1,0:T(8,128)(2,1)S(1)}, bf16[256,1792]{1,0:T(8,128)(2,1)S(1)}, u32[]{:S(2)}, u32[]{:S(2)}) collective-permute-start(bf16[256,1792]{1,0:T(8,128)(2,1)S(1)} %add_convert_fusion.4), channel_id=1, source_target_pairs={{0,4},{4,0},{8,12},{12,8},{1,5},{5,1},{9,13},{13,9},{2,6},{6,2},{1... | collective-permute-start | bytes 2752520 | tf_op jit(solution)/shard_map/ppermute | solution.py:147
  262.9 19.8 %collective-permute-start.8 = (bf16[256,1792]{1,0:T(8,128)(2,1)S(1)}, bf16[256,1792]{1,0:T(8,128)(2,1)S(1)}, u32[]{:S(2)}, u32[]{:S(2)}) collective-permute-start(bf16[256,1792]{1,0:T(8,128)(2,1)S(1)} %add_convert_fusion.2), channel_id=1, source_target_pairs={{0,4},{4,0},{8,12},{12,8},{1,5},{5,1},{9,13},{13,9},{2,6},{6,2},{1... | collective-permute-start | bytes 2752520 | tf_op jit(solution)/shard_map/ppermute | solution.py:147
  282.1 2.5 collective-permute-start.11
  285.9 2.9 copy-start.1
  288.8 25.2 %collective-permute-start.12 = (f32[256,1024]{1,0:T(8,128)S(1)}, f32[256,1024]{1,0:T(8,128)S(1)}, u32[]{:S(2)}, u32[]{:S(2)}) collective-permute-start(f32[256,1024]{1,0:T(8,128)S(1)} %fusion.1), channel_id=1, source_target_pairs={{0,1},{1,0},{2,3},{3,2},{4,5},{5,4},{6,7},{7,6},{8,9},{9,8},{10,11... | collective-permute-start | bytes 3145736 | tf_op jit(solution)/shard_map/ppermute | solution.py:147
  314.2 47.5 %collective-permute-start.13 = (f32[256,1024]{1,0:T(8,128)S(1)}, f32[256,1024]{1,0:T(8,128)S(1)}, u32[]{:S(2)}, u32[]{:S(2)}) collective-permute-start(f32[256,1024]{1,0:T(8,128)S(1)} %add.52), channel_id=1, source_target_pairs={{0,2},{1,3},{2,0},{3,1},{4,6},{5,7},{6,4},{7,5},{8,10},{9,11},{10,... | collective-permute-start | bytes 3145736 | tf_op jit(solution)/shard_map/ppermute | solution.py:147
  396.6 2.2 copy-start
  398.8 68.5 %slice-start = ((s8[7340032]{0:T(1024)(128)(4,1)}), s8[3145728]{0:T(1024)(128)(4,1)S(1)}, s32[]{:S(2)}) async-start(s8[7340032]{0:T(1024)(128)(4,1)} %bitcast.27), calls=%async_computation.5 | async-start | bytes 6291456
  461.9 5.4 %slice-start.1 = ((s8[7340032]{0:T(1024)(128)(4,1)}), s8[4194304]{0:T(1024)(128)(4,1)S(1)}, s32[]{:S(2)}) async-start(s8[7340032]{0:T(1024)(128)(4,1)} %bitcast.27), calls=%async_computation.6 | async-start | bytes 8388608
Sparse Core Ops, SparseCore 0:
  10.8 44.0 all-gather.5
  56.5 40.2 all-gather.7
  98.4 40.2 all-gather.9
  140.2 40.2 all-gather.11
  363.0 33.5 all-gather.13

commit v2 on v1

--- a/solution.py
+++ b/solution.py
@@ -13,6 +13,7 @@
 STEP = 8
 PANEL = 32
 EXACT = lax.Precision.HIGHEST
+COST = 10**10
 
 
 def dot_rows(x, y):
@@ -30,7 +31,6 @@
     column = lax.broadcasted_iota(jnp.int32, shape, 1)
     left = [block[8 * i : 8 * i + 8, :] for i in range(pieces)]
     right = [jnp.where(column == row + 8 * i, 1.0, 0.0).astype(jnp.float32) for i in range(pieces)]
-    diagonal = jnp.zeros(shape, jnp.float32)
 
     def spread(value):
         return jnp.broadcast_to(value, shape)
@@ -71,7 +71,6 @@
                     right[i] = right[i] - columns[s][i] * solved_sides[s]
         for s in range(STEP):
             root = lax.rsqrt(corner[s][s])
-            diagonal = jnp.where(column == first + s, corner[s][s] * root, diagonal)
             left[own] = jnp.where(row == s, rows[s] * root, left[own])
             right[own] = jnp.where(row == s, sides[s] * root, right[own])
         if (first + STEP) % PANEL == 0 and first + STEP < BLOCK:
@@ -82,20 +81,17 @@
             for i in range(end, pieces):
                 left[i] = left[i] - update[8 * i : 8 * i + 8, :BLOCK]
                 right[i] = right[i] - update[8 * i : 8 * i + 8, BLOCK:]
-    return right, diagonal[:1]
-
-
-def factor_kernel(gram_ref, high_ref, low_ref, scales_ref, work):
-    size = gram_ref.shape[0]
-    blocks = size // BLOCK
-    work[...] = gram_ref[...]
+    return right
+
+
+def eliminate(work, first, last):
+    blocks = work.shape[0] // BLOCK
     one = lax.broadcasted_iota(jnp.int32, (BLOCK, BLOCK), 0) == lax.broadcasted_iota(jnp.int32, (BLOCK, BLOCK), 1)
 
-    @pl.loop(0, blocks)
+    @pl.loop(first, last)
     def _(j):
         own = pl.ds(pl.multiple_of(j * BLOCK, BLOCK), BLOCK)
-        pieces, diagonal = factor_block(work[own, own])
-        scales_ref[:, own] = diagonal
+        pieces = factor_block(work[own, own])
         work[own, own] = jnp.where(one, 1.0, 0.0).astype(jnp.float32)
         work[own, :] = dot_plain(jnp.concatenate(pieces, axis=0), work[own, :])
 
@@ -106,29 +102,203 @@
             work[other, own] = jnp.zeros((BLOCK, BLOCK), jnp.float32)
             work[other, :] = work[other, :] - dot_rows(upper, work[own, :])
 
+
+def lower_part(value):
+    row = lax.broadcasted_iota(jnp.int32, value.shape, 0)
+    return jnp.where(lax.broadcasted_iota(jnp.int32, value.shape, 1) <= row, value, 0.0)
+
+
+def pairs_of(n):
+    return [(0, False)] + [(d, 2 * d == n) for d in range(1, n // 2 + 1)]
+
+
+def own_pair(r, offset, n):
+    if 2 * offset == n:
+        low = r % offset
+        return low, low + offset
+    other = (r + offset) % n
+    return jnp.minimum(r, other), jnp.maximum(r, other)
+
+
+def place_symmetric(matrix, held, n, block):
+    for r in range(n):
+        row = 0
+        for offset, split in pairs_of(n):
+            if split:
+                i, j = r % offset, r % offset + offset
+                height, start = block // 2, r // offset * (block // 2)
+            else:
+                i, j = min(r, (r + offset) % n), max(r, (r + offset) % n)
+                height, start = block, 0
+            matrix[i * block + start : i * block + start + height, j * block : (j + 1) * block] = held(
+                r, row, height
+            )
+            row += height
+    return row
+
+
+def first_kernel(n, order, steps, r_ref, *refs):
+    held, work, stack = refs[:n], refs[n], refs[n + 1]
+    size = work.shape[0]
+    r = r_ref[0]
+    for value, distance in zip(held, order):
+        stack[r ^ distance] = value[...]
+    work[...] = jnp.zeros_like(work)
+    place_symmetric(work, lambda d, row, height: stack[d, row : row + height, :], n, size // n)
+    eliminate(work, 0, steps)
+
+
+def second_kernel(steps, before_ref, work):
+    work[...] = before_ref[...]
+    eliminate(work, steps, work.shape[0] // BLOCK)
+
+
+def last_kernel(n, order, r_ref, *refs):
+    held, left_ref = refs[:n], refs[n]
+    high_ref, low_ref, scales_ref, stack, whole, cross, work = refs[n + 1 :]
+    size = left_ref.shape[0]
+    block = size // n
+    r = r_ref[0]
+    for value, distance in zip(held, order):
+        stack[r ^ distance] = value[...]
+    corner = place_symmetric(work, lambda d, row, height: stack[d, row : row + height, :], n, block)
+    for d in range(n):
+        for j in range(n):
+            cross[d * block : (d + 1) * block, j * block : (j + 1) * block] = stack[
+                d, corner + j * block : corner + (j + 1) * block, :
+            ]
+    inverse = lower_part(left_ref[...])
+    whole[:size, :size] = inverse
+    whole[:size, size:] = jnp.zeros((size, size), jnp.float32)
+    cross[...] = dot_plain(inverse, cross[...])
     row = lax.broadcasted_iota(jnp.int32, (size, size), 0)
     column = lax.broadcasted_iota(jnp.int32, (size, size), 1)
-    full = jnp.where(column <= row, work[...], 0.0)
-    high = full.astype(jnp.bfloat16)
+    upper = jnp.where(row // block <= column // block, work[...], 0.0)
+    work[...] = upper - dot_rows(cross[...], cross[...])
+    eliminate(work, 0, size // BLOCK)
+    inverse = lower_part(work[...])
+    whole[size:, size:] = inverse
+    whole[size:, :size] = -dot_plain(inverse, dot_rows(cross[...], whole[:size, :size]))
+    one = lax.broadcasted_iota(jnp.int32, (BLOCK, BLOCK), 0) == lax.broadcasted_iota(jnp.int32, (BLOCK, BLOCK), 1)
+    for first in range(0, 2 * size, BLOCK):
+        at = slice(first, first + BLOCK)
+        scales_ref[:, at] = 1.0 / jnp.sum(jnp.where(one, whole[at, at], 0.0), axis=0, keepdims=True)
+    portion = high_ref.shape[0]
+    rows = whole[pl.ds(pl.multiple_of(r * portion, portion), portion), :]
+    high = rows.astype(jnp.bfloat16)
     high_ref[...] = high
-    low_ref[...] = (full - high.astype(jnp.float32)).astype(jnp.bfloat16)
-
-
-def invert_factor(gram):
-    size = gram.shape[0]
-    vmem = pl.BlockSpec(memory_space=pltpu.VMEM)
+    low_ref[...] = (rows - high.astype(jnp.float32)).astype(jnp.bfloat16)
+
+
+VMEM = pl.BlockSpec(memory_space=pltpu.VMEM)
+SMEM = pl.BlockSpec(memory_space=pltpu.SMEM)
+
+
+def kernel_options():
+    return {
+        "compiler_params": pltpu.CompilerParams(vmem_limit_bytes=40 * 2**20),
+        "cost_estimate": pl.CostEstimate(flops=COST, bytes_accessed=0, transcendentals=0),
+    }
+
+
+def invert_factor(index, order, corner, rest, size):
+    n = len(order)
+    half = size // 2
+    square = jax.ShapeDtypeStruct((half, half), jnp.float32)
+    steps = half // BLOCK // 2
+    work = pl.pallas_call(
+        functools.partial(first_kernel, n, order, steps),
+        out_shape=square,
+        in_specs=[SMEM] + [VMEM] * n,
+        out_specs=VMEM,
+        scratch_shapes=[pltpu.VMEM((n,) + corner[0].shape, jnp.float32)],
+        **kernel_options(),
+    )(index, *corner)
+    work = pl.pallas_call(
+        functools.partial(second_kernel, steps),
+        out_shape=square,
+        in_specs=[VMEM],
+        out_specs=VMEM,
+        **kernel_options(),
+    )(work)
+    portion = size // n
     return pl.pallas_call(
-        factor_kernel,
+        functools.partial(last_kernel, n, order),
         out_shape=[
-            jax.ShapeDtypeStruct((size, size), jnp.bfloat16),
-            jax.ShapeDtypeStruct((size, size), jnp.bfloat16),
+            jax.ShapeDtypeStruct((portion, size), jnp.bfloat16),
+            jax.ShapeDtypeStruct((portion, size), jnp.bfloat16),
             jax.ShapeDtypeStruct((1, size), jnp.float32),
         ],
-        in_specs=[vmem],
-        out_specs=[vmem] * 3,
-        scratch_shapes=[pltpu.VMEM((size, size), jnp.float32)],
+        in_specs=[SMEM] + [VMEM] * (n + 1),
+        out_specs=[VMEM] * 3,
+        scratch_shapes=[
+            pltpu.VMEM((n,) + rest[0].shape, jnp.float32),
+            pltpu.VMEM((size, size), jnp.float32),
+            pltpu.VMEM((half, half), jnp.float32),
+            pltpu.VMEM((half, half), jnp.float32),
+        ],
+        **kernel_options(),
+    )(index, *rest, work)
+
+
+def multiply_kernel(layout, tile, which_ref, *refs):
+    candidates, factor_ref, out_ref = refs[:-6], refs[-6], refs[-5]
+    block, weights, block_ready, ready = refs[-4:]
+    half = out_ref.shape[2]
+    tiles = half // tile
+    core = which_ref[0]
+    places = []
+    for i in range(2 * tiles):
+        part = lax.rem(i // tiles + core + 1, 2)
+        places.append(pl.ds(pl.multiple_of(part * half + i % tiles * tile, tile), tile))
+    first, row = 0, 0
+    for piece, count in enumerate(layout):
+        height = candidates[first].shape[0]
+        for k in range(count):
+
+            @pl.when(which_ref[piece + 1] == k)
+            def _(k=k, first=first, row=row, height=height, piece=piece):
+                pltpu.make_async_copy(
+                    candidates[first + k], block.at[pl.ds(row, height)], block_ready.at[piece]
+                ).start()
+
+        first, row = first + count, row + height
+    copies = [pltpu.make_async_copy(factor_ref.at[p], weights.at[i], ready.at[i]) for i, p in enumerate(places)]
+    for copy in copies:
+        copy.start()
+    first, row = 0, 0
+    for piece, count in enumerate(layout):
+        height = candidates[first].shape[0]
+        pltpu.make_async_copy(candidates[first], block.at[pl.ds(row, height)], block_ready.at[piece]).wait()
+        first, row = first + count, row + height
+    for i, copy in enumerate(copies):
+        copy.wait()
+        out_ref[i // tiles, :, i % tiles * tile : (i % tiles + 1) * tile] = lax.dot_general(
+            block[...], weights[i], (((1,), (1,)), ((), ())), preferred_element_type=jnp.float32
+        )
+
+
+def multiply(which, pieces, factor):
+    rows, depth = factor.shape
+    columns = sum(candidates[0].shape[0] for candidates in pieces)
+    half = rows // 2
+    tile = next((t for t in (896, 512, 256) if half % t == 0), half)
+    tiles = 2 * half // tile
+    layout = tuple(len(candidates) for candidates in pieces)
+    return pl.pallas_call(
+        functools.partial(multiply_kernel, layout, tile),
+        in_specs=[pl.BlockSpec(memory_space=pltpu.SMEM)] + [pl.BlockSpec(memory_space=pl.ANY)] * (sum(layout) + 1),
+        out_specs=pl.BlockSpec(memory_space=pltpu.VMEM),
+        scratch_shapes=[
+            pltpu.VMEM((columns, depth), jnp.bfloat16),
+            pltpu.VMEM((tiles, tile, depth), jnp.bfloat16),
+            pltpu.SemaphoreType.DMA((len(layout),)),
+            pltpu.SemaphoreType.DMA((tiles,)),
+        ],
+        out_shape=jax.ShapeDtypeStruct((2, columns, half), jnp.float32),
         compiler_params=pltpu.CompilerParams(vmem_limit_bytes=40 * 2**20),
-    )(gram)
+        cost_estimate=pl.CostEstimate(flops=COST, bytes_accessed=0, transcendentals=0),
+    )(which, *[c for candidates in pieces for c in candidates], factor)
 
 
 def local(factor, basis_rows):
@@ -136,10 +306,9 @@
     own_basis = basis_rows.shape[0]
     n_row, n_col = lax.axis_size("row"), lax.axis_size("col")
     basis = own_basis * n_col
-    chunks = max(1, min(4, own_basis // 16))
-    height = own_basis // chunks
     half = rows // 2
     index = lax.axis_index("row")
+    plane = lax.axis_index("col")
     core = index % 2
 
     def exchange(value, axis, distance):
@@ -147,13 +316,22 @@
         return lax.ppermute(value, axis, [(i, i ^ distance) for i in range(size)])
 
     rounded = basis_rows.astype(jnp.bfloat16)
-    parts = []
-    for k in range(chunks):
-        gathered = lax.all_gather(rounded[k * height : (k + 1) * height], "col", axis=0, tiled=True)
-        partial = lax.dot_general(gathered, factor, (((1,), (1,)), ((), ())), preferred_element_type=jnp.float32)
-        kept = jnp.where(core == 0, partial[:, :half], partial[:, half:])
-        given = jnp.where(core == 0, partial[:, half:], partial[:, :half])
-        total = kept + exchange(given, "row", 1)
+    cut = own_basis // 2
+
+    def stream(part):
+        below, above = [part], [part]
+        for hop in range(1, n_col):
+            below.append(lax.ppermute(below[-1], "col", [(i, i + 1) for i in range(hop - 1, n_col - 1)]))
+            above.append(lax.ppermute(above[-1], "col", [(i + 1, i) for i in range(0, n_col - hop)]))
+        return below, above
+
+    halves = [jnp.zeros((basis, half), jnp.bfloat16)] * 2
+
+    def add_unit(halves, pieces):
+        blocks = [jnp.where(hop <= plane, plane - hop, hop) for hop, _, _ in pieces]
+        which = jnp.stack([core] + [jnp.where(hop <= plane, 0, hop - plane) for hop, _, _ in pieces])
+        products = multiply(which.astype(jnp.int32), [candidates for _, _, candidates in pieces], factor)
+        total = products[1] + exchange(products[0], "row", 1)
         distance = 2
         while distance < n_row:
             narrow = total.astype(jnp.bfloat16)
@@ -161,23 +339,82 @@
             distance *= 2
         total = total.astype(jnp.bfloat16)
         other = exchange(total, "row", 1)
-        full = jnp.concatenate(
-            [jnp.where(core == 0, total, other), jnp.where(core == 0, other, total)], axis=1
+        row = 0
+        for (_, offset, candidates), block in zip(pieces, blocks):
+            height = candidates[0].shape[0]
+            start = block * own_basis + offset
+            halves = [
+                lax.dynamic_update_slice_in_dim(h, v[row : row + height], start, 0)
+                for h, v in zip(halves, (total, other))
+            ]
+            row += height
+        return halves
+
+    halves = add_unit(halves, [(0, 0, [rounded])])
+    streams = []
+    for offset, part in ((0, rounded[:cut]), (cut, rounded[cut:])):
+        below, above = stream(part)
+        streams.append([(hop, offset, [below[hop]] + above[1 : hop + 1]) for hop in range(1, n_col)])
+    units = [list(pair) for pair in zip(*streams)]
+    units = units[:-1] + [[piece] for piece in units[-1]]
+    for unit in units:
+        halves = add_unit(halves, unit)
+
+    side = basis // 2
+    block = side // n_row
+
+    def gram(rows, columns):
+        return sum(
+            lax.dot_general(
+                lax.dynamic_slice_in_dim(h, rows[0], rows[1], 0),
+                lax.dynamic_slice_in_dim(h, columns[0], columns[1], 0),
+                (((1,), (1,)), ((), ())),
+                preferred_element_type=jnp.float32,
+            )
+            for h in halves
         )
-        parts.append(full.reshape(n_col, height, rows))
-    products = jnp.stack(parts, axis=1).reshape(basis, rows)
-
-    portion = basis // n_row
-    own_part = lax.dynamic_slice_in_dim(products, index * portion, portion, 0)
-    gram = lax.dot_general(own_part, products, (((1,), (1,)), ((), ())), preferred_element_type=jnp.float32)
-    distance = 1
-    while distance < n_col:
-        gram = gram + exchange(gram, "col", distance)
-        distance *= 2
-    gram = lax.all_gather(gram, "row", axis=0, tiled=True)
-    high, low, scales = invert_factor(gram)
-    high = lax.dynamic_slice_in_dim(high, index * portion, portion, 0)
-    low = lax.dynamic_slice_in_dim(low, index * portion, portion, 0)
+
+    def share(start):
+        found = []
+        for offset, split in pairs_of(n_row):
+            i, j = own_pair(index, offset, n_row) if offset else (index, index)
+            height = block // 2 if split else block
+            first = start + i * block + (index // offset * height if split else 0)
+            found.append(gram((first, height), (start + j * block, block)))
+        return found
+
+    corner = jnp.concatenate(share(0), axis=0)
+    cross = gram((index * block, block), (side, side))
+    rest = jnp.concatenate(share(side) + [cross[:, j * block : (j + 1) * block] for j in range(n_row)], axis=0)
+
+    def over_planes(value):
+        if n_col == 4:
+            toward = lax.ppermute(value, "col", [(0, 1), (3, 2)])
+            value = value + toward
+            value = value + lax.ppermute(value, "col", [(1, 2), (2, 1)])
+            outward = lax.ppermute(value, "col", [(1, 0), (2, 3)])
+            return jnp.where((plane == 0) | (plane == 3), outward, value)
+        distance = 1
+        while distance < n_col:
+            value = value + exchange(value, "col", distance)
+            distance *= 2
+        return value
+
+    def over_row(value):
+        held = {0: value}
+        distances = [1 << k for k in range(1, n_row.bit_length() - 1)] + [1]
+        for distance in distances:
+            held |= {d ^ distance: exchange(v, "row", distance) for d, v in held.items()}
+        return held
+
+    corner, rest = over_row(over_planes(corner)), over_row(over_planes(rest))
+    order = tuple(corner)
+    high, low, scales = invert_factor(
+        index.reshape(1).astype(jnp.int32), order, list(corner.values()), list(rest.values()), basis
+    )
+    first = jnp.where(core == 0, halves[0], halves[1])
+    second = jnp.where(core == 0, halves[1], halves[0])
+    products = jnp.concatenate([first, second], axis=1)
     new_basis = lax.dot_general(
         products, high, (((0,), (1,)), ((), ())), preferred_element_type=jnp.float32
     ) + lax.dot_general(products, low, (((0,), (1,)), ((), ())), preferred_element_type=jnp.float32)

time: 478 us -> 308 us (0.64); the launches traced: 478 us -> 302 us
  waiting for transfers between devices: 294 us -> 111 us
  Pallas kernels: 63.1 us -> 119 us
  matrix products: 66.8 us -> 12 us
  starting transfers between devices: 6.76 us -> 41.2 us
  other arithmetic: 28.6 us -> 8.19 us
  between operations: 14 us -> 1.67 us
    all_gather x5 -> x0, waiting for transfers between devices: 149 us -> none  [the longest x4 115 us: local(): lax.all_gather(rounded[k * height:(k + 1) * height], 'col', axis=0, tiled...]
    ppermute x14 -> x21, waiting for transfers between devices: 143 us -> 36.8 us  [exchange(): return lax.ppermute(value, axis, [(i, i ^ distance) for i in range(size)])]
    ppermute x0 -> x18, waiting for transfers between devices: none -> 74.7 us  [the longest x6 34.7 us: stream(): lax.ppermute(above[-1], 'col', [(i + 1, i) for i in range(0, n_col - hop)])]
    pallas_call x1 -> x8, Pallas kernels: 63.1 us -> 119 us  [the longest x5 61.9 us: multiply(): pl.pallas_call(functools.partial(multiply_kernel, layout, tile), in_specs...]
    dot_general x5 -> x14, matrix products: 57.4 us -> 4.9 us  [gram(): lax.dot_general(lax.dynamic_slice_in_dim(h, rows[0], rows[1], 0), lax.dyn...]
    ppermute x0 -> x18, starting transfers between devices: none -> 29.2 us  [the longest x6 14.2 us: stream(): lax.ppermute(below[-1], 'col', [(i, i + 1) for i in range(hop - 1, n_col...]
    select_n x8 -> x3, other arithmetic: 14.6 us -> 3.7 us  [the longest x1 3.64 us: local(): first = jnp.where(core == 0, halves[0], halves[1])]
    convert_element_type x8 -> x7, other arithmetic: 9.06 us -> 1.31 us  [the longest x5 0.88 us: add_unit(): narrow = total.astype(jnp.bfloat16)]
  transfers between devices with their start and end apart: 19 -> 39, of which waited for: 12 -> 14; matrix products, arithmetic and copies ran while one was open for 17% -> 4% of each run, Pallas kernels for 0% -> 29%
where the time goes in v2:
time: 308 us; the launch traced here: 302 us
  Pallas kernels  119 us (39%)
  waiting for transfers between devices  111 us (36%)
  starting transfers between devices  41.2 us (13%)
  matrix products  12 us (4%)
  local copies, waits for them, and re-layouts  8.54 us (3%)
  other arithmetic  8.19 us (3%)
    pallas_call x5, Pallas kernels, multiply(): pl.pallas_call(functools.partial(multiply_kernel, layout, tile), in_specs...  61.9 us
    ppermute x21, waiting for transfers between devices, exchange(): return lax.ppermute(value, axis, [(i, i ^ distance) for i in range(size)])  36.8 us
    ppermute x6, waiting for transfers between devices, stream(): lax.ppermute(above[-1], 'col', [(i + 1, i) for i in range(0, n_col - hop)])  34.7 us
    pallas_call x1, Pallas kernels, invert_factor(): pl.pallas_call(functools.partial(last_kernel, n, order), out_shape=[jax.S...  32.5 us
    ppermute x2, waiting for transfers between devices, over_planes(): outward = lax.ppermute(value, 'col', [(1, 0), (2, 3)])  16.9 us
    ppermute x6, starting transfers between devices, stream(): lax.ppermute(below[-1], 'col', [(i, i + 1) for i in range(hop - 1, n_col...  14.2 us
    pallas_call x1, Pallas kernels, invert_factor(): pl.pallas_call(functools.partial(first_kernel, n, order, steps), out_shap...  13 us
    ppermute x21, starting transfers between devices, exchange(): return lax.ppermute(value, axis, [(i, i ^ distance) for i in range(size)])  12 us
  transfers between devices with their start and end apart: 39, of which 14 were waited for; matrix products, arithmetic and copies ran while one was open for 4% of the time, Pallas kernels for 29%

profile of v2, /device:TPU:0, one launch (start us, length us, event | category | flops | bytes accessed | tf_op | source)
XLA Modules:
  0.0 301.8 jit_solution(3999285435814728250)
XLA Ops:
  0.6 2.2 convert_element_type.63.refs_0_
  4.2 5.9 %collective-permute-start.2 = (bf16[128,3584]{1,0:T(8,128)(2,1)}, bf16[128,3584]{1,0:T(8,128)(2,1)}, u32[]{:S(2)}, u32[]{:S(2)}) collective-permute-start(bf16[128,3584]{1,0:T(8,128)(2,1)} %get-tuple-element.17), channel_id=1, source_target_pairs={{0,1},{1,2},{2,3},{4,5},{5,6},{6,7},{8,9},{9,10},{10,11},{12,13},{... | collective-permute-start | bytes 2752520 | tf_op jit(solution)/shard_map/ppermute | solution.py:324
  11.4 5.5 %collective-permute-start.4 = (bf16[128,3584]{1,0:T(8,128)(2,1)}, bf16[128,3584]{1,0:T(8,128)(2,1)}, u32[]{:S(2)}, u32[]{:S(2)}) collective-permute-start(bf16[128,3584]{1,0:T(8,128)(2,1)} %get-tuple-element.16), channel_id=1, source_target_pairs={{0,1},{1,2},{2,3},{4,5},{5,6},{6,7},{8,9},{9,10},{10,11},{12,13},{... | collective-permute-start | bytes 2752520 | tf_op jit(solution)/shard_map/ppermute | solution.py:324
  18.3 11.9 %shard_map.41 = f32[2,256,1792]{2,1,0:T(8,128)S(1)} custom-call(s32[2]{0:T(128)S(1)} %pad_add_fusion.which_ref, bf16[256,3584]{1,0:T(8,128)(2,1)S(1)} %convert_element_type.63.refs_0_, bf16[3584,3584]{1,0:T(8,128)(2,1)} %refs_4_.5), custom_call_target="tpu_custom_call" | custom-call | flops 10000000000 | tf_op jit(solution)/shard_map/pallas_call | solution.py:288
  30.2 1.8 copy-done
  36.9 11.8 %collective-permute-done.4.refs_2_ = bf16[128,3584]{1,0:T(8,128)(2,1)} collective-permute-done((bf16[128,3584]{1,0:T(8,128)(2,1)}, bf16[128,3584]{1,0:T(8,128)(2,1)}, u32[]{:S(2)}, u32[]{:S(2)}) %collective-permute-start.4) | collective-permute-done | bytes 917536 | tf_op jit(solution)/shard_map/ppermute | solution.py:324
  49.4 5.7 %collective-permute-done.5.refs_3_.refs_4_.refs_1_ = bf16[128,3584]{1,0:T(8,128)(2,1)S(1)} collective-permute-done((bf16[128,3584]{1,0:T(8,128)(2,1)}, bf16[128,3584]{1,0:T(8,128)(2,1)S(1)}, u32[]{:S(2)}, u32[]{:S(2)}) %collective-permute-start.5) | collective-permute-done | bytes 917536 | tf_op jit(solution)/shard_map/ppermute | solution.py:325
  56.4 12.2 %shard_map.42 = f32[2,256,1792]{2,1,0:T(8,128)S(1)} custom-call(s32[3]{0:T(128)S(1)} %pad_add_fusion.1.which_ref, bf16[128,3584]{1,0:T(8,128)(2,1)} %collective-permute-done.2.refs_0_, bf16[128,3584]{1,0:T(8,128)(2,1)} %collective-permute-done.3.refs_1_, bf16[128,3584]{1,0:T(8,128)(2,1)} %collective-permute-done.4.refs_2_, ...), custom_call_target="tpu_custom_call" | custom-call | flops 10000000000 | tf_op jit(solution)/shard_map/pallas_call | solution.py:288
  71.7 1.6 collective-permute-start.1
  73.2 1.6 collective-permute-done.9.refs_2_
  76.8 17.6 %collective-permute-done.11.refs_5_.refs_2_ = bf16[128,3584]{1,0:T(8,128)(2,1)S(1)} collective-permute-done((bf16[128,3584]{1,0:T(8,128)(2,1)S(1)}, bf16[128,3584]{1,0:T(8,128)(2,1)S(1)}, u32[]{:S(2)}, u32[]{:S(2)}) %collective-permute-start.11) | collective-permute-done | bytes 917536 | tf_op jit(solution)/shard_map/ppermute | solution.py:325
  94.5 12.2 %shard_map.43 = f32[2,256,1792]{2,1,0:T(8,128)S(1)} custom-call(s32[3]{0:T(128)S(1)} %pad_add_fusion.2.which_ref, bf16[128,3584]{1,0:T(8,128)(2,1)S(1)} %collective-permute-done.8.refs_0_, bf16[128,3584]{1,0:T(8,128)(2,1)} %collective-permute-done.3.refs_1_, bf16[128,3584]{1,0:T(8,128)(2,1)S(1)} %collective-permute-done.9.refs_2_, ...), custom_call_target="tpu_custom_call" | custom-call | flops 10000000000 | tf_op jit(solution)/shard_map/pallas_call | solution.py:288
  107.9 1.7 collective-permute-start.19
  109.6 3.1 %collective-permute-done.15.refs_3_ = bf16[128,3584]{1,0:T(8,128)(2,1)S(1)} collective-permute-done((bf16[128,3584]{1,0:T(8,128)(2,1)S(1)}, bf16[128,3584]{1,0:T(8,128)(2,1)S(1)}, u32[]{:S(2)}, u32[]{:S(2)}) %collective-permute-start.15) | collective-permute-done | bytes 917536 | tf_op jit(solution)/shard_map/ppermute | solution.py:325
  114.2 12.8 %shard_map.44 = f32[2,128,1792]{2,1,0:T(8,128)S(1)} custom-call(s32[2]{0:T(128)S(1)} %pad_add_fusion.3.which_ref, bf16[128,3584]{1,0:T(8,128)(2,1)S(1)} %collective-permute-done.14.refs_0_, bf16[128,3584]{1,0:T(8,128)(2,1)} %collective-permute-done.3.refs_1_, bf16[128,3584]{1,0:T(8,128)(2,1)S(1)} %collective-permute-done.9.refs_2_, ...), custom_call_target="tpu_custom_call" | custom-call | flops 10000000000 | tf_op jit(solution)/shard_map/pallas_call | solution.py:288
  127.1 5.4 %collective-permute-done.19.refs_3_ = bf16[128,3584]{1,0:T(8,128)(2,1)S(1)} collective-permute-done((bf16[128,3584]{1,0:T(8,128)(2,1)S(1)}, bf16[128,3584]{1,0:T(8,128)(2,1)S(1)}, u32[]{:S(2)}, u32[]{:S(2)}) %collective-permute-start.19) | collective-permute-done | bytes 917536 | tf_op jit(solution)/shard_map/ppermute | solution.py:325
  132.5 12.8 %shard_map.45 = f32[2,128,1792]{2,1,0:T(8,128)S(1)} custom-call(s32[2]{0:T(128)S(1)} %pad_add_fusion.3.which_ref, bf16[128,3584]{1,0:T(8,128)(2,1)S(1)} %collective-permute-done.18.refs_0_, bf16[128,3584]{1,0:T(8,128)(2,1)S(1)} %collective-permute-done.5.refs_3_.refs_4_.refs_1_, bf16[128,3584]{1,0:T(8,128)(2,1)S(1)} %collective-permute-done.11.refs_5_.refs_2_, ...), custom_call_target="tpu_custom_call" | custom-call | flops 10000000000 | tf_op jit(solution)/shard_map/pallas_call | solution.py:288
  146.8 1.5 collective-permute-start.13
  149.2 1.5 collective-permute-start.21
  151.5 18.6 %collective-permute-done.13 = bf16[256,1792]{1,0:T(8,128)(2,1)S(1)} collective-permute-done((bf16[256,1792]{1,0:T(8,128)(2,1)S(1)}, bf16[256,1792]{1,0:T(8,128)(2,1)S(1)}, u32[]{:S(2)}, u32[]{:S(2)}) %collective-permute-start.13) | collective-permute-done | bytes 917536 | tf_op jit(solution)/shard_map/ppermute | solution.py:316
  170.5 9.4 %collective-permute-done.17 = bf16[128,1792]{1,0:T(8,128)(2,1)S(1)} collective-permute-done((bf16[128,1792]{1,0:T(8,128)(2,1)S(1)}, bf16[128,1792]{1,0:T(8,128)(2,1)S(1)}, u32[]{:S(2)}, u32[]{:S(2)}) %collective-permute-start.17) | collective-permute-done | bytes 458784 | tf_op jit(solution)/shard_map/ppermute | solution.py:316
  180.1 8.7 %collective-permute-done.21 = bf16[128,1792]{1,0:T(8,128)(2,1)S(1)} collective-permute-done((bf16[128,1792]{1,0:T(8,128)(2,1)S(1)}, bf16[128,1792]{1,0:T(8,128)(2,1)S(1)}, u32[]{:S(2)}, u32[]{:S(2)}) %collective-permute-start.21) | collective-permute-done | bytes 458784 | tf_op jit(solution)/shard_map/ppermute | solution.py:316
  197.2 3.1 %collective-permute-done.33 = f32[320,128]{1,0:T(8,128)S(1)} collective-permute-done((f32[320,128]{1,0:T(8,128)S(1)}, f32[320,128]{1,0:T(8,128)S(1)}, u32[]{:S(2)}, u32[]{:S(2)}) %collective-permute-start.33) | collective-permute-done | bytes 163872 | tf_op jit(solution)/shard_map/ppermute | solution.py:392
  201.1 8.2 %collective-permute-done.27 = f32[832,128]{1,0:T(8,128)S(1)} collective-permute-done((f32[832,128]{1,0:T(8,128)S(1)}, f32[832,128]{1,0:T(8,128)S(1)}, u32[]{:S(2)}, u32[]{:S(2)}) %collective-permute-start.27) | collective-permute-done | bytes 426016 | tf_op jit(solution)/shard_map/ppermute | solution.py:392
  211.3 7.9 %collective-permute-done.35 = f32[320,128]{1,0:T(8,128)S(1)} collective-permute-done((f32[320,128]{1,0:T(8,128)S(1)}, f32[320,128]{1,0:T(8,128)S(1)}, u32[]{:S(2)}, u32[]{:S(2)}) %collective-permute-start.35) | collective-permute-done | bytes 163872 | tf_op jit(solution)/shard_map/ppermute | solution.py:395
  222.3 3.6 %broadcast_select_fusion.1 = (bf16[1024,1792]{1,0:T(8,128)(2,1)S(1)}, bf16[1024,1792]{1,0:T(8,128)(2,1)S(1)}) fusion(bf16[1024,1792]{1,0:T(8,128)(2,1)} %copy-done.3, bf16[1024,1792]{1,0:T(8,128)(2,1)} %copy-done.2, pred[]{:T(512)S(6)} %eq.18), kind=kLoop, calls=%fused_computation.5 | loop fusion | flops 3670016 | bytes 14680065 | tf_op jit(solution)/shard_map/jit(_where)/select_n | solution.py:415
  226.5 9.0 %collective-permute-done.29 = f32[832,128]{1,0:T(8,128)S(1)} collective-permute-done((f32[832,128]{1,0:T(8,128)S(1)}, f32[832,128]{1,0:T(8,128)S(1)}, u32[]{:S(2)}, u32[]{:S(2)}) %collective-permute-start.29) | collective-permute-done | bytes 426016 | tf_op jit(solution)/shard_map/ppermute | solution.py:395
  237.1 13.0 %shard_map.46.before_ref = f32[512,512]{1,0:T(8,128)S(1)} custom-call(s32[1]{0:T(128)} %bitcast.15.r_ref, f32[320,128]{1,0:T(8,128)S(1)} %broadcast_select_fusion.3.refs_0_, f32[320,128]{1,0:T(8,128)S(1)} %collective-permute-done.36.refs_1_, f32[320,128]{1,0:T(8,128)S(1)} %collective-permute-done.37.refs_2_, f32[320,128]{1,0:T(8,128)S(1)} %collective-permute-done.38.refs_3_), custom_call_target="tpu_custom_call" | custom-call | flops 10000000000 | tf_op jit(solution)/shard_map/pallas_call | solution.py:209
  250.7 11.2 %shard_map.47.refs_4_ = f32[512,512]{1,0:T(8,128)S(1)} custom-call(f32[512,512]{1,0:T(8,128)S(1)} %shard_map.46.before_ref), custom_call_target="tpu_custom_call" | custom-call | flops 10000000000 | tf_op jit(solution)/shard_map/pallas_call | solution.py:217
  262.0 32.5 %shard_map.48 = (bf16[256,1024]{1,0:T(8,128)(2,1)S(1)}, bf16[256,1024]{1,0:T(8,128)(2,1)S(1)}, f32[1,1024]{1,0:T(1,128)}) custom-call(s32[1]{0:T(128)} %bitcast.15.r_ref, f32[832,128]{1,0:T(8,128)S(1)} %broadcast_select_fusion.2.refs_0_, f32[832,128]{1,0:T(8,128)S(1)} %collective-permute-done.30.refs_1_, f32[832,128]{1,0:T(8,128)S(1)} %collective-permute-done.31.refs_2_, ...), custom_call_target="tpu_custom_call" | custom-call | flops 10000000000 | tf_op jit(solution)/shard_map/pallas_call | solution.py:225
  294.5 2.3 fusion.1
  296.8 4.8 %fusion = f32[3584,256]{1,0:T(8,128)} fusion(f32[3584,256]{1,0:T(8,128)S(1)} %fusion.1, bf16[256,1024]{1,0:T(8,128)(2,1)S(1)} %get-tuple-element.5, bf16[1024,1792]{1,0:T(8,128)(2,1)S(1)} %get-tuple-element.15, bf16[1024,1792]{1,0:T(8,128)(2,1)S(1)} %get-tuple-element.14), kind=kOutput, calls=%fused_computation.2 | convolution fusion | flops 1895563264 | bytes 15204352 | tf_op jit(solution)/shard_map/dot_general | solution.py:418
  (124 shorter events, 38.7 us)
Async XLA Ops:
  4.2 29.4 %collective-permute-start.2 = (bf16[128,3584]{1,0:T(8,128)(2,1)}, bf16[128,3584]{1,0:T(8,128)(2,1)}, u32[]{:S(2)}, u32[]{:S(2)}) collective-permute-start(bf16[128,3584]{1,0:T(8,128)(2,1)} %get-tuple-element.17), channel_id=1, source_target_pairs={{0,1},{1,2},{2,3},{4,5},{5,6},{6,7},{8,9},{9,10},{10,11},{12,13},{... | collective-permute-start | bytes 2752520 | tf_op jit(solution)/shard_map/ppermute | solution.py:324
  10.1 25.5 %collective-permute-start.3 = (bf16[128,3584]{1,0:T(8,128)(2,1)}, bf16[128,3584]{1,0:T(8,128)(2,1)}, u32[]{:S(2)}, u32[]{:S(2)}) collective-permute-start(bf16[128,3584]{1,0:T(8,128)(2,1)} %get-tuple-element.17), channel_id=1, source_target_pairs={{1,0},{2,1},{3,2},{5,4},{6,5},{7,6},{9,8},{10,9},{11,10},{13,12},{... | collective-permute-start | bytes 2752520 | tf_op jit(solution)/shard_map/ppermute | solution.py:325
  11.4 37.3 %collective-permute-start.4 = (bf16[128,3584]{1,0:T(8,128)(2,1)}, bf16[128,3584]{1,0:T(8,128)(2,1)}, u32[]{:S(2)}, u32[]{:S(2)}) collective-permute-start(bf16[128,3584]{1,0:T(8,128)(2,1)} %get-tuple-element.16), channel_id=1, source_target_pairs={{0,1},{1,2},{2,3},{4,5},{5,6},{6,7},{8,9},{9,10},{10,11},{12,13},{... | collective-permute-start | bytes 2752520 | tf_op jit(solution)/shard_map/ppermute | solution.py:324
  16.9 38.2 %collective-permute-start.5 = (bf16[128,3584]{1,0:T(8,128)(2,1)}, bf16[128,3584]{1,0:T(8,128)(2,1)S(1)}, u32[]{:S(2)}, u32[]{:S(2)}) collective-permute-start(bf16[128,3584]{1,0:T(8,128)(2,1)} %get-tuple-element.16), channel_id=1, source_target_pairs={{1,0},{2,1},{3,2},{5,4},{6,5},{7,6},{9,8},{10,9},{11,10},{13,12},{... | collective-permute-start | bytes 2752520 | tf_op jit(solution)/shard_map/ppermute | solution.py:325
  33.4 36.7 %collective-permute-start = (f32[256,1792]{1,0:T(8,128)}, f32[256,1792]{1,0:T(8,128)S(1)}, u32[]{:S(2)}, u32[]{:S(2)}) collective-permute-start(f32[256,1792]{1,0:T(8,128)} %slice_bitcast_fusion.4), channel_id=1, source_target_pairs={{0,4},{4,0},{8,12},{12,8},{1,5},{5,1},{9,13},{13,9},{2,6},{6,2},{1... | collective-permute-start | bytes 5505032 | tf_op jit(solution)/shard_map/ppermute | solution.py:316
  33.7 38.0 %collective-permute-start.8 = (bf16[128,3584]{1,0:T(8,128)(2,1)}, bf16[128,3584]{1,0:T(8,128)(2,1)S(1)}, u32[]{:S(2)}, u32[]{:S(2)}) collective-permute-start(bf16[128,3584]{1,0:T(8,128)(2,1)} %collective-permute-done.2.refs_0_), channel_id=1, source_target_pairs={{1,2},{2,3},{5,6},{6,7},{9,10},{10,11},{13,14},{14,15},{17,18},{18... | collective-permute-start | bytes 2752520 | tf_op jit(solution)/shard_map/ppermute | solution.py:324
  35.6 39.2 %collective-permute-start.9 = (bf16[128,3584]{1,0:T(8,128)(2,1)}, bf16[128,3584]{1,0:T(8,128)(2,1)S(1)}, u32[]{:S(2)}, u32[]{:S(2)}) collective-permute-start(bf16[128,3584]{1,0:T(8,128)(2,1)} %collective-permute-done.3.refs_1_), channel_id=1, source_target_pairs={{1,0},{2,1},{5,4},{6,5},{9,8},{10,9},{13,12},{14,13},{17,16},{18,1... | collective-permute-start | bytes 2752520 | tf_op jit(solution)/shard_map/ppermute | solution.py:325
  48.7 26.8 %collective-permute-start.10 = (bf16[128,3584]{1,0:T(8,128)(2,1)}, bf16[128,3584]{1,0:T(8,128)(2,1)S(1)}, u32[]{:S(2)}, u32[]{:S(2)}) collective-permute-start(bf16[128,3584]{1,0:T(8,128)(2,1)} %collective-permute-done.4.refs_2_), channel_id=1, source_target_pairs={{1,2},{2,3},{5,6},{6,7},{9,10},{10,11},{13,14},{14,15},{17,18},{18... | collective-permute-start | bytes 2752520 | tf_op jit(solution)/shard_map/ppermute | solution.py:324
  55.2 39.3 %collective-permute-start.11 = (bf16[128,3584]{1,0:T(8,128)(2,1)S(1)}, bf16[128,3584]{1,0:T(8,128)(2,1)S(1)}, u32[]{:S(2)}, u32[]{:S(2)}) collective-permute-start(bf16[128,3584]{1,0:T(8,128)(2,1)S(1)} %collective-permute-done.5.refs_3_.refs_4_.refs_1_), channel_id=1, source_target_pairs={{1,0},{2,1},{5,4},{6,5},{9,8},{10,9},{13,12},{14,13},{17,16},{18,1... | collective-permute-start | bytes 2752520 | tf_op jit(solution)/shard_map/ppermute | solution.py:325
  70.1 36.9 %collective-permute-start.6 = (f32[256,1792]{1,0:T(8,128)}, f32[256,1792]{1,0:T(8,128)S(1)}, u32[]{:S(2)}, u32[]{:S(2)}) collective-permute-start(f32[256,1792]{1,0:T(8,128)} %slice_bitcast_fusion.2), channel_id=1, source_target_pairs={{0,4},{4,0},{8,12},{12,8},{1,5},{5,1},{9,13},{13,9},{2,6},{6,2},{1... | collective-permute-start | bytes 5505032 | tf_op jit(solution)/shard_map/ppermute | solution.py:316
  71.7 73.8 %collective-permute-start.1 = (bf16[256,1792]{1,0:T(8,128)(2,1)S(1)}, bf16[256,1792]{1,0:T(8,128)(2,1)S(1)}, u32[]{:S(2)}, u32[]{:S(2)}) collective-permute-start(bf16[256,1792]{1,0:T(8,128)(2,1)S(1)} %fusion.11), channel_id=1, source_target_pairs={{0,8},{4,12},{8,0},{12,4},{1,9},{5,13},{9,1},{13,5},{2,10},{6,14},... | collective-permute-start | bytes 2752520 | tf_op jit(solution)/shard_map/ppermute | solution.py:316
  74.8 33.1 %collective-permute-start.14 = (bf16[128,3584]{1,0:T(8,128)(2,1)S(1)}, bf16[128,3584]{1,0:T(8,128)(2,1)S(1)}, u32[]{:S(2)}, u32[]{:S(2)}) collective-permute-start(bf16[128,3584]{1,0:T(8,128)(2,1)S(1)} %collective-permute-done.8.refs_0_), channel_id=1, source_target_pairs={{2,3},{6,7},{10,11},{14,15},{18,19},{22,23},{26,27},{30,31}} | collective-permute-start | bytes 2752520 | tf_op jit(solution)/shard_map/ppermute | solution.py:324
  75.5 37.1 %collective-permute-start.15 = (bf16[128,3584]{1,0:T(8,128)(2,1)S(1)}, bf16[128,3584]{1,0:T(8,128)(2,1)S(1)}, u32[]{:S(2)}, u32[]{:S(2)}) collective-permute-start(bf16[128,3584]{1,0:T(8,128)(2,1)S(1)} %collective-permute-done.9.refs_2_), channel_id=1, source_target_pairs={{1,0},{5,4},{9,8},{13,12},{17,16},{21,20},{25,24},{29,28}} | collective-permute-start | bytes 2752520 | tf_op jit(solution)/shard_map/ppermute | solution.py:325
  106.9 39.7 %collective-permute-start.12 = (f32[256,1792]{1,0:T(8,128)S(1)}, f32[256,1792]{1,0:T(8,128)S(1)}, u32[]{:S(2)}, u32[]{:S(2)}) collective-permute-start(f32[256,1792]{1,0:T(8,128)S(1)} %slice_bitcast_fusion), channel_id=1, source_target_pairs={{0,4},{4,0},{8,12},{12,8},{1,5},{5,1},{9,13},{13,9},{2,6},{6,2},{1... | collective-permute-start | bytes 5505032 | tf_op jit(solution)/shard_map/ppermute | solution.py:316
  107.0 20.1 %collective-permute-start.18 = (bf16[128,3584]{1,0:T(8,128)(2,1)S(1)}, bf16[128,3584]{1,0:T(8,128)(2,1)S(1)}, u32[]{:S(2)}, u32[]{:S(2)}) collective-permute-start(bf16[128,3584]{1,0:T(8,128)(2,1)S(1)} %collective-permute-done.10.refs_3_), channel_id=1, source_target_pairs={{2,3},{6,7},{10,11},{14,15},{18,19},{22,23},{26,27},{30,31}} | collective-permute-start | bytes 2752520 | tf_op jit(solution)/shard_map/ppermute | solution.py:324
  107.9 24.6 %collective-permute-start.19 = (bf16[128,3584]{1,0:T(8,128)(2,1)S(1)}, bf16[128,3584]{1,0:T(8,128)(2,1)S(1)}, u32[]{:S(2)}, u32[]{:S(2)}) collective-permute-start(bf16[128,3584]{1,0:T(8,128)(2,1)S(1)} %collective-permute-done.11.refs_5_.refs_2_), channel_id=1, source_target_pairs={{1,0},{5,4},{9,8},{13,12},{17,16},{21,20},{25,24},{29,28}} | collective-permute-start | bytes 2752520 | tf_op jit(solution)/shard_map/ppermute | solution.py:325
  112.7 38.0 %collective-permute-start.7 = (bf16[256,1792]{1,0:T(8,128)(2,1)S(1)}, bf16[256,1792]{1,0:T(8,128)(2,1)S(1)}, u32[]{:S(2)}, u32[]{:S(2)}) collective-permute-start(bf16[256,1792]{1,0:T(8,128)(2,1)S(1)} %fusion.9), channel_id=1, source_target_pairs={{0,8},{4,12},{8,0},{12,4},{1,9},{5,13},{9,1},{13,5},{2,10},{6,14},... | collective-permute-start | bytes 2752520 | tf_op jit(solution)/shard_map/ppermute | solution.py:316
  127.0 21.3 %collective-permute-start.16 = (f32[128,1792]{1,0:T(8,128)S(1)}, f32[128,1792]{1,0:T(8,128)S(1)}, u32[]{:S(2)}, u32[]{:S(2)}) collective-permute-start(f32[128,1792]{1,0:T(8,128)S(1)} %slice_bitcast_fusion.8), channel_id=1, source_target_pairs={{0,4},{4,0},{8,12},{12,8},{1,5},{5,1},{9,13},{13,9},{2,6},{6,2},{1... | collective-permute-start | bytes 2752520 | tf_op jit(solution)/shard_map/ppermute | solution.py:316
  146.8 23.3 %collective-permute-start.13 = (bf16[256,1792]{1,0:T(8,128)(2,1)S(1)}, bf16[256,1792]{1,0:T(8,128)(2,1)S(1)}, u32[]{:S(2)}, u32[]{:S(2)}) collective-permute-start(bf16[256,1792]{1,0:T(8,128)(2,1)S(1)} %fusion.7), channel_id=1, source_target_pairs={{0,8},{4,12},{8,0},{12,4},{1,9},{5,13},{9,1},{13,5},{2,10},{6,14},... | collective-permute-start | bytes 2752520 | tf_op jit(solution)/shard_map/ppermute | solution.py:316
  148.4 31.5 %collective-permute-start.17 = (bf16[128,1792]{1,0:T(8,128)(2,1)S(1)}, bf16[128,1792]{1,0:T(8,128)(2,1)S(1)}, u32[]{:S(2)}, u32[]{:S(2)}) collective-permute-start(bf16[128,1792]{1,0:T(8,128)(2,1)S(1)} %fusion.21), channel_id=1, source_target_pairs={{0,8},{4,12},{8,0},{12,4},{1,9},{5,13},{9,1},{13,5},{2,10},{6,14},... | collective-permute-start | bytes 1376264 | tf_op jit(solution)/shard_map/ppermute | solution.py:316
  149.2 39.6 %collective-permute-start.21 = (bf16[128,1792]{1,0:T(8,128)(2,1)S(1)}, bf16[128,1792]{1,0:T(8,128)(2,1)S(1)}, u32[]{:S(2)}, u32[]{:S(2)}) collective-permute-start(bf16[128,1792]{1,0:T(8,128)(2,1)S(1)} %fusion.19), channel_id=1, source_target_pairs={{0,8},{4,12},{8,0},{12,4},{1,9},{5,13},{9,1},{13,5},{2,10},{6,14},... | collective-permute-start | bytes 1376264 | tf_op jit(solution)/shard_map/ppermute | solution.py:316
  150.9 39.8 %collective-permute-start.23 = (bf16[256,1792]{1,0:T(8,128)(2,1)S(1)}, bf16[256,1792]{1,0:T(8,128)(2,1)S(1)}, u32[]{:S(2)}, u32[]{:S(2)}) collective-permute-start(bf16[256,1792]{1,0:T(8,128)(2,1)S(1)} %add_convert_fusion.1), channel_id=1, source_target_pairs={{0,4},{4,0},{8,12},{12,8},{1,5},{5,1},{9,13},{13,9},{2,6},{6,2},{1... | collective-permute-start | bytes 2752520 | tf_op jit(solution)/shard_map/ppermute | solution.py:316
  170.3 20.6 %collective-permute-start.24 = (bf16[256,1792]{1,0:T(8,128)(2,1)S(1)}, bf16[256,1792]{1,0:T(8,128)(2,1)S(1)}, u32[]{:S(2)}, u32[]{:S(2)}) collective-permute-start(bf16[256,1792]{1,0:T(8,128)(2,1)S(1)} %add_convert_fusion), channel_id=1, source_target_pairs={{0,4},{4,0},{8,12},{12,8},{1,5},{5,1},{9,13},{13,9},{2,6},{6,2},{1... | collective-permute-start | bytes 2752520 | tf_op jit(solution)/shard_map/ppermute | solution.py:316
  180.0 11.0 %collective-permute-start.25 = (bf16[128,1792]{1,0:T(8,128)(2,1)S(1)}, bf16[128,1792]{1,0:T(8,128)(2,1)S(1)}, u32[]{:S(2)}, u32[]{:S(2)}) collective-permute-start(bf16[128,1792]{1,0:T(8,128)(2,1)S(1)} %get-tuple-element.11), channel_id=1, source_target_pairs={{0,4},{4,0},{8,12},{12,8},{1,5},{5,1},{9,13},{13,9},{2,6},{6,2},{1... | collective-permute-start | bytes 1376264 | tf_op jit(solution)/shard_map/ppermute | solution.py:316
  195.9 13.3 %collective-permute-start.27 = (f32[832,128]{1,0:T(8,128)S(1)}, f32[832,128]{1,0:T(8,128)S(1)}, u32[]{:S(2)}, u32[]{:S(2)}) collective-permute-start(f32[832,128]{1,0:T(8,128)S(1)} %slice_dynamic-update-slice_fusion.8), channel_id=1, source_target_pairs={{0,1},{3,2},{4,5},{7,6},{8,9},{11,10},{12,13},{15,14},{16,17},{19,... | collective-permute-start | bytes 1277960 | tf_op jit(solution)/shard_map/ppermute | solution.py:392
  209.3 11.5 %collective-permute-start.28 = (f32[832,128]{1,0:T(8,128)S(1)}, f32[832,128]{1,0:T(8,128)S(1)}, u32[]{:S(2)}, u32[]{:S(2)}) collective-permute-start(f32[832,128]{1,0:T(8,128)S(1)} %add.247), channel_id=1, source_target_pairs={{1,2},{2,1},{5,6},{6,5},{9,10},{10,9},{13,14},{14,13},{17,18},{18,... | collective-permute-start | bytes 1277960 | tf_op jit(solution)/shard_map/ppermute | solution.py:394
  220.8 14.7 %collective-permute-start.29 = (f32[832,128]{1,0:T(8,128)S(1)}, f32[832,128]{1,0:T(8,128)S(1)}, u32[]{:S(2)}, u32[]{:S(2)}) collective-permute-start(f32[832,128]{1,0:T(8,128)S(1)} %add.248), channel_id=1, source_target_pairs={{1,0},{2,3},{5,4},{6,7},{9,8},{10,11},{13,12},{14,15},{17,16},{18,... | collective-permute-start | bytes 1277960 | tf_op jit(solution)/shard_map/ppermute | solution.py:395
  226.0 11.2 %collective-permute-start.37 = (f32[320,128]{1,0:T(8,128)S(1)}, f32[320,128]{1,0:T(8,128)S(1)}, u32[]{:S(2)}, u32[]{:S(2)}) collective-permute-start(f32[320,128]{1,0:T(8,128)S(1)} %broadcast_select_fusion.3.refs_0_), channel_id=1, source_target_pairs={{0,4},{4,0},{8,12},{12,8},{1,5},{5,1},{9,13},{13,9},{2,6},{6,2},{1... | collective-permute-start | bytes 491528 | tf_op jit(solution)/shard_map/ppermute | solution.py:316
  226.0 11.1 %collective-permute-start.38 = (f32[320,128]{1,0:T(8,128)S(1)}, f32[320,128]{1,0:T(8,128)S(1)}, u32[]{:S(2)}, u32[]{:S(2)}) collective-permute-start(f32[320,128]{1,0:T(8,128)S(1)} %collective-permute-done.36.refs_1_), channel_id=1, source_target_pairs={{0,4},{4,0},{8,12},{12,8},{1,5},{5,1},{9,13},{13,9},{2,6},{6,2},{1... | collective-permute-start | bytes 491528 | tf_op jit(solution)/shard_map/ppermute | solution.py:316
  235.6 14.6 %collective-permute-start.30 = (f32[832,128]{1,0:T(8,128)S(1)}, f32[832,128]{1,0:T(8,128)S(1)}, u32[]{:S(2)}, u32[]{:S(2)}) collective-permute-start(f32[832,128]{1,0:T(8,128)S(1)} %broadcast_select_fusion.2.refs_0_), channel_id=1, source_target_pairs={{0,8},{4,12},{8,0},{12,4},{1,9},{5,13},{9,1},{13,5},{2,10},{6,14},... | collective-permute-start | bytes 1277960 | tf_op jit(solution)/shard_map/ppermute | solution.py:316
  250.1 11.8 %collective-permute-start.31 = (f32[832,128]{1,0:T(8,128)S(1)}, f32[832,128]{1,0:T(8,128)S(1)}, u32[]{:S(2)}, u32[]{:S(2)}) collective-permute-start(f32[832,128]{1,0:T(8,128)S(1)} %broadcast_select_fusion.2.refs_0_), channel_id=1, source_target_pairs={{0,4},{4,0},{8,12},{12,8},{1,5},{5,1},{9,13},{13,9},{2,6},{6,2},{1... | collective-permute-start | bytes 1277960 | tf_op jit(solution)/shard_map/ppermute | solution.py:316
  250.2 11.7 %collective-permute-start.32 = (f32[832,128]{1,0:T(8,128)S(1)}, f32[832,128]{1,0:T(8,128)S(1)}, u32[]{:S(2)}, u32[]{:S(2)}) collective-permute-start(f32[832,128]{1,0:T(8,128)S(1)} %collective-permute-done.30.refs_1_), channel_id=1, source_target_pairs={{0,4},{4,0},{8,12},{12,8},{1,5},{5,1},{9,13},{13,9},{2,6},{6,2},{1... | collective-permute-start | bytes 1277960 | tf_op jit(solution)/shard_map/ppermute | solution.py:316
  (11 other events, 53.1 us)
